TPU v7x, 768 devices: a whole 4x8x12 slice. The times are simulated.
768 devices in a mesh: slab: 96 (over z, x, core), cross: 8 (over y).
Axes of the slice: x: 4, y: 8, z: 12, core: 2. Of those that a mesh axis runs over, the one named last changes fastest.
Arguments:
- fields: bfloat16 [4, 192, 8, 16, 8, 256], P(None, 'slab', None, 'cross'), may hold values from -1.796875 to 1.796875
- sep_factor: float32 [192, 16, 33, 1024], P('slab', 'cross'), may hold values from -0.03125 to 0.03125
- local_factor: float32 [192, 16, 33, 132], P('slab', 'cross'), may hold values from -0.3125 to 0.3125
Outputs:
- conv_rate: float32 [4, 192, 8, 16, 8, 256], P(None, 'slab', None, 'cross')
- pressure: float32 [192, 16, 33], P('slab', 'cross')
All inputs are finite; a program needn't handle non-finite values.
Results may differ from a plain program's by a relative error of at most 0.0004.
Values sent between devices are 32-bit elements; how exact they have to be, the bound alone decides.
No kernel may reach another device: no remote copies, remote signals or barrier semaphores. Data moves between devices by JAX's collectives and lax.ppermute only.
A program may use at most 128 MiB of HBM per device.

v0:
```python
import functools

import jax
import jax.numpy as jnp
import numpy as np
from jax import lax
from jax.experimental import pallas as pl
from jax.experimental.pallas import tpu as pltpu
from jax.sharding import Mesh
from jax.sharding import PartitionSpec as P

degree = 7
step_size = 0.25
bf16 = jnp.bfloat16
f32 = jnp.float32


def legendre_values(order, points):
    earlier = points * 0.0 + 1.0
    current = points * 1.0
    for level_index in range(1, order):
        follow = ((2 * level_index + 1) * points * current - level_index * earlier) / (
            level_index + 1
        )
        earlier = current
        current = follow
    return current


def tables():
    gll_nodes = np.array(
        [
            -1.0,
            -0.8717401485096066,
            -0.5917001814331423,
            -0.2092992179024789,
            0.2092992179024789,
            0.5917001814331423,
            0.8717401485096066,
            1.0,
        ]
    )
    at_nodes = legendre_values(degree, gll_nodes)
    weights = 2.0 / (degree * (degree + 1) * at_nodes**2)
    points = degree + 1
    derivative = np.zeros((points, points))
    for target in range(points):
        for source in range(points):
            if target != source:
                derivative[target, source] = at_nodes[target] / (
                    at_nodes[source] * (gll_nodes[target] - gll_nodes[source])
                )
    derivative[0, 0] = -degree * (degree + 1) / 4.0
    derivative[-1, -1] = degree * (degree + 1) / 4.0
    half_nodes = np.array(
        [
            0.1252334085114689,
            0.3678314989981802,
            0.5873179542866175,
            0.7699026741943047,
            0.9041172563704749,
            0.9815606342467192,
        ]
    )
    fine_nodes = np.concatenate([-half_nodes[::-1], half_nodes])
    for newton_step in range(3):
        top_value = legendre_values(12, fine_nodes)
        below_value = legendre_values(11, fine_nodes)
        slope_value = (
            12.0 * (fine_nodes * top_value - below_value) / (fine_nodes * fine_nodes - 1.0)
        )
        fine_nodes = fine_nodes - top_value / slope_value
    top_value = legendre_values(12, fine_nodes)
    below_value = legendre_values(11, fine_nodes)
    slope_value = 12.0 * (fine_nodes * top_value - below_value) / (fine_nodes * fine_nodes - 1.0)
    fine_weights = 2.0 / ((1.0 - fine_nodes * fine_nodes) * slope_value * slope_value)
    interp = np.ones((12, points))
    for source in range(points):
        for target in range(points):
            if target != source:
                interp[:, source] *= (fine_nodes - gll_nodes[target]) / (
                    gll_nodes[source] - gll_nodes[target]
                )
    slope_interp = interp @ derivative
    vertex_hats = np.stack([(1.0 - gll_nodes) / 2.0, (1.0 + gll_nodes) / 2.0]) * weights[None, :]
    return weights, derivative, interp, slope_interp, fine_weights, vertex_hats


def halves(matrix):
    high = matrix.astype(np.float32).astype(jnp.bfloat16)
    low = (matrix - high.astype(np.float64)).astype(np.float32).astype(jnp.bfloat16)
    return high, low


def split(x):
    high = x.astype(bf16)
    return high, (x - high.astype(f32)).astype(bf16)


def constants(ez):
    weights, derivative, interp, slope_interp, fine_weights, hats = tables()
    eye = np.eye(ez)
    spread = np.concatenate([np.kron(eye, interp.T), np.kron(eye, slope_interp.T)], axis=1)
    spread = np.concatenate(halves(spread), axis=0)
    lift = np.concatenate(
        [np.kron(interp, interp), np.kron(slope_interp, interp), np.kron(interp, slope_interp)]
    )
    high, low = halves(lift)
    lift = np.concatenate([high, low, high, low], axis=1)
    across = weights.copy()
    across[0] = across[7] = weights[0] + weights[7]
    back = interp.T * fine_weights[None, :]
    fall = -np.kron(back / across[:, None], back / across[:, None])
    high, low = halves(fall)
    fall = np.concatenate([high, high, low], axis=1)
    joined = np.eye(8 * ez)
    for at in range(ez - 1):
        joined[8 * at + 7, 8 * at + 8] = joined[8 * at + 8, 8 * at + 7] = 1.0
    mass = joined @ np.tile(weights, ez)
    gather = np.kron(eye, back.T) @ joined / mass[None, :]
    high, low = halves(gather)
    gather = np.concatenate([high, high, low], axis=0)
    own, rise = [], []
    slope_hats = hats @ derivative
    for f in range(3):
        own_pair, wide_pair = [], []
        for d in range(2):
            hat = slope_hats if f == d else hats
            rows = 8 if d else 5
            plain = np.zeros((rows, 16))
            for e in range(2):
                for a in range(2):
                    plain[e + a + 1, 8 * e : 8 * e + 8] += hat[a]
            shared = plain.copy()
            for a in range(2):
                shared[a, 0] += hat[a, 7]
                shared[3 + a, 15] += hat[a, 0]
            own_pair.append(plain)
            wide_pair.append(shared)
        own_high, own_low = halves(np.kron(*own_pair))
        wide_high, wide_low = halves(step_size * np.kron(*wide_pair))
        own.append(np.concatenate([own_high, own_low, wide_high, wide_high, wide_low], axis=1))
        hat = slope_hats if f == 2 else hats
        up = np.zeros((8 * ez, 128))
        for e in range(ez):
            for a in range(2):
                up[8 * e : 8 * e + 8, e + a] += hat[a]
        high, low = halves(up)
        rise.append(np.concatenate([high, high, low], axis=0))
    return spread, lift, fall, gather, np.stack(own), np.stack(rise)


def first_kernel(
    fields, spread, lift, fall, gather, own, rise, out, low_x, high_x, low_y, high_y, hold, points, down
):
    nodes = fields[...].astype(f32).reshape(1024, 256).astype(bf16)
    points[...] = jnp.dot(
        jnp.concatenate([nodes, nodes], axis=1), spread[...], preferred_element_type=f32
    ).reshape(points.shape)

    def column(at, carry):
        ex = lax.div(at, 2)
        ey = lax.rem(at, 2)
        speeds = []
        slopes = []
        for f in range(4):
            values = points[f, ex, :, ey].reshape(64, 768)
            high, low = split(values)
            stacked = jnp.concatenate([high, high, low, low], axis=0)
            first = jnp.dot(lift[...], stacked[:, :384], preferred_element_type=f32)
            second = jnp.dot(lift[:144], stacked[:, 384:], preferred_element_type=f32)
            if f < 3:
                speeds.append(first[:144])
            slopes.append((first[144:288], first[288:], second))
        for f in range(4):
            product = sum(speeds[d] * slopes[f][d] for d in range(3))
            high, low = split(product)
            stacked = jnp.concatenate([high, low, high], axis=0)
            fallen = jnp.dot(fall[...], stacked, preferred_element_type=f32)
            down[f, ex, :, ey] = fallen.reshape(8, 8, 384)
        return carry

    lax.fori_loop(0, 4, column, 0)
    high, low = split(down[...].reshape(1024, 384))
    stacked = jnp.concatenate([high, low, high], axis=1)
    out[...] = jnp.dot(stacked, gather[...], preferred_element_type=f32).reshape(out.shape)
    middle = out[:, 0, 7] + out[:, 1, 0]
    out[:, 0, 7] = middle
    out[:, 1, 0] = middle
    middle = out[:, :, :, 0, 7:8] + out[:, :, :, 1, 0:1]
    out[:, :, :, 0, 7:8] = middle
    out[:, :, :, 1, 0:1] = middle
    low_x[:64] = out[:, 0, 0].reshape(64, 256)
    high_x[:64] = out[:, 1, 7].reshape(64, 256)
    low_y[...] = out[:, :, :, 0, 0].reshape(64, 256)
    high_y[...] = out[:, :, :, 1, 7].reshape(64, 256)
    total = jnp.zeros((40, 128), f32)
    for f in range(3):
        high, low = split(out[f].reshape(256, 256))
        part = nodes[256 * f : 256 * (f + 1)]
        stacked = jnp.concatenate([part, part, high, low, high], axis=0)
        flat = jnp.dot(own[f], stacked, preferred_element_type=f32)
        high, low = split(flat)
        total = total + jnp.dot(
            jnp.concatenate([high, low, high], axis=1), rise[f], preferred_element_type=f32
        )
    low_x[64:, :128] = total[:8]
    low_x[64:, 128:] = jnp.zeros((8, 128), f32)
    high_x[64:, :128] = total[24:32]
    high_x[64:, 128:] = total[32:]
    hold[...] = total[8:24]


def second_kernel(from_low, from_high, low_y, high_y, hold, low_out, high_out, hold_out):
    low_out[:64] = low_y[...]
    high_out[:64] = high_y[...]
    for f in range(4):
        first, last = 16 * f, 16 * f + 15
        low_out[first : first + 1] = low_y[first : first + 1] + from_low[first : first + 1]
        low_out[last : last + 1] = low_y[last : last + 1] + from_high[first : first + 1]
        high_out[first : first + 1] = high_y[first : first + 1] + from_low[last : last + 1]
        high_out[last : last + 1] = high_y[last : last + 1] + from_high[last : last + 1]
    near = hold[:8] + from_low[64:, :128]
    far = hold[8:] + from_low[64:, 128:] + from_high[64:, :128]
    hold_out[:8] = near
    hold_out[8:] = far
    low_out[64:, :128] = near
    low_out[64:, 128:] = far
    high_out[64:, :128] = near
    high_out[64:, 128:] = far


def third_kernel(
    partial, low_x, high_x, low_y, high_y, hold, sep, inner, out, sums, term
):
    out[...] = partial[...]
    out[:, 0, 0] = out[:, 0, 0] + low_x[:64].reshape(4, 2, 8, 256)
    out[:, 1, 7] = out[:, 1, 7] + high_x[:64].reshape(4, 2, 8, 256)
    out[:, :, :, 0, 0] = out[:, :, :, 0, 0] + low_y[:64].reshape(4, 2, 8, 256)
    out[:, :, :, 1, 7] = out[:, :, :, 1, 7] + high_y[:64].reshape(4, 2, 8, 256)
    rows = []
    for vx in range(2):
        side = slice(128 * vx, 128 * vx + 128)
        rows.append(hold[8 * vx + 1 : 8 * vx + 2] + low_y[67:68, side])
        rows.append(
            hold[8 * vx + 2 : 8 * vx + 3] + low_y[68:69, side] + high_y[64:65, side]
        )
    upright = jnp.transpose(jnp.concatenate(rows + rows, axis=0))
    columns = [upright[:33, v : v + 1] for v in range(4)]
    for at in range(8):
        lanes = slice(128 * at, 128 * at + 128)
        total = sum(columns[v] * sep[v // 2, v % 2, :, lanes] for v in range(4))
        total = jnp.sum(total, axis=0, keepdims=True)
        sums[at : at + 1] = total
    total = sum(columns[v] * inner[v // 2, v % 2] for v in range(4))
    total = jnp.sum(total, axis=0, keepdims=True)
    for v in range(4):
        term[v // 2, v % 2 : v % 2 + 1] = lax.dot_general(
            total, inner[v // 2, v % 2], (((1,), (1,)), ((), ())),
            precision=lax.Precision.HIGHEST, preferred_element_type=f32,
        )


def last_kernel(arrived, sep, term, out):
    total = jnp.sum(arrived[...], axis=0)
    ones = jnp.ones((1, 128), f32)
    for v in range(4):
        spread_out = sum(
            sep[v // 2, v % 2, :, 128 * at : 128 * at + 128] * total[at : at + 1] for at in range(8)
        )
        out[v // 2, v % 2 : v % 2 + 1] = term[v // 2, v % 2 : v % 2 + 1] + lax.dot_general(
            ones, spread_out, (((1,), (1,)), ((), ())),
            precision=lax.Precision.HIGHEST, preferred_element_type=f32,
        )


def call(kernel, shapes, arrays, scratch=(), **options):
    whole = pl.BlockSpec(memory_space=pltpu.VMEM)
    return pl.pallas_call(
        kernel,
        out_shape=[jax.ShapeDtypeStruct(s, f32) for s in shapes],
        in_specs=[whole] * len(arrays),
        out_specs=[whole] * len(shapes),
        scratch_shapes=[pltpu.VMEM(s, f32) for s in scratch],
        compiler_params=pltpu.CompilerParams(vmem_limit_bytes=48 * 2**20),
        **options,
    )(*arrays)


def first(fields):
    tabs = [jnp.asarray(t) for t in constants(fields.shape[5] // 8)]
    return call(
        first_kernel,
        [fields.shape, (72, 256), (72, 256), (64, 256), (64, 256), (16, 128)],
        [fields] + tabs,
        [(4, 2, 8, 2, 8, 768), (4, 2, 8, 2, 8, 384)],
    )


def shifted(x, axis, by):
    count = lax.axis_size(axis)
    return lax.ppermute(x, axis, [(i, (i + by) % count) for i in range(count)])


slab = ("z", "x", "core")


def scattered(tile, axis):
    count = lax.axis_size(axis)
    return lax.all_to_all(jnp.broadcast_to(tile, (count,) + tile.shape), axis, 0, 0)


def local(fields, sep_factor, local_factor):
    partial, low_x, high_x, low_y, high_y, hold = first(fields)
    from_high = shifted(low_x, slab, -1)
    from_low = shifted(high_x, slab, 1)
    low_y, high_y, hold = call(
        second_kernel, [(72, 256), (72, 256), (16, 128)], [from_low, from_high, low_y, high_y, hold]
    )
    y_high = shifted(low_y, "cross", -1)
    y_low = shifted(high_y, "cross", 1)
    conv_rate, sums, term = call(
        third_kernel,
        [fields.shape, (8, 128), (2, 2, 33)],
        [partial, from_low, from_high, y_low, y_high, hold, sep_factor, local_factor],
    )
    sums = jnp.sum(scattered(sums, ("x", "core")), axis=0)
    sums = jnp.sum(scattered(sums, "cross"), axis=0)
    sums = scattered(sums, "z")
    pressure = call(last_kernel, [(2, 2, 33)], [sums, sep_factor, term])[0]
    return conv_rate, pressure


def solution(mesh):
    fine = Mesh(mesh.devices.reshape(12, 4, 2, 8), ("z", "x", "core", "cross"))
    return jax.shard_map(
        local,
        mesh=fine,
        in_specs=(
            P(None, slab, None, "cross", None, None),
            P(slab, "cross", None, None),
            P(slab, "cross", None, None),
        ),
        out_specs=(P(None, slab, None, "cross", None, None), P(slab, "cross", None)),
        check_vma=False,
    )
```

profile of v0, /device:TPU:1, one launch (start us, length us, event | category | flops | bytes accessed | tf_op | source)
XLA Modules:
  0.0 85.9 jit_solution(16081058881521244180)
XLA Ops:
  0.6 0.0 copy-start
  0.6 1.1 %copy-done = bf16[512,768]{1,0:T(8,128)(2,1)S(1)} copy-done((bf16[512,768]{1,0:T(8,128)(2,1)S(1)}, bf16[512,768]{1,0:T(8,128)(2,1)}, u32[]{:S(2)}) %copy-start) | copy-done | bytes 786456
  1.8 0.0 copy-start.1
  1.8 1.1 %copy-done.1 = bf16[3,768,128]{2,1,0:T(8,128)(2,1)S(1)} copy-done((bf16[3,768,128]{2,1,0:T(8,128)(2,1)S(1)}, bf16[3,768,128]{2,1,0:T(8,128)(2,1)}, u32[]{:S(2)}) %copy-start.1) | copy-done | bytes 589848
  2.8 0.0 copy-start.2
  2.8 1.1 %copy-done.2 = bf16[1152,256]{1,0:T(8,128)(2,1)S(1)} copy-done((bf16[1152,256]{1,0:T(8,128)(2,1)S(1)}, bf16[1152,256]{1,0:T(8,128)(2,1)}, u32[]{:S(2)}) %copy-start.2) | copy-done | bytes 589848
  3.9 0.0 copy-start.3
  3.9 1.0 %copy-done.3 = bf16[4,2,8,2,8,256]{5,4,3,2,1,0:T(8,128)(2,1)S(1)} copy-done((bf16[4,2,8,2,8,256]{5,4,3,2,1,0:T(8,128)(2,1)S(1)}, bf16[4,2,8,2,8,256]{5,4,3,2,1,0:T(8,128)(2,1)}, u32[]{:S(2)}) %copy-start.3) | copy-done | bytes 524312
  4.9 0.0 copy-start.4
  4.9 1.0 %copy-done.4 = bf16[3,40,1280]{2,1,0:T(8,128)(2,1)S(1)} copy-done((bf16[3,40,1280]{2,1,0:T(8,128)(2,1)S(1)}, bf16[3,40,1280]{2,1,0:T(8,128)(2,1)}, u32[]{:S(2)}) %copy-start.4) | copy-done | bytes 307224
  5.9 0.0 copy-start.5
  5.9 0.9 %copy-done.5 = bf16[432,256]{1,0:T(8,128)(2,1)S(1)} copy-done((bf16[432,256]{1,0:T(8,128)(2,1)S(1)}, bf16[432,256]{1,0:T(8,128)(2,1)}, u32[]{:S(2)}) %copy-start.5) | copy-done | bytes 221208
  6.8 0.0 copy-start.6
  6.8 0.8 copy-done.6
  7.7 0.0 copy-start.8
  7.7 7.1 %shard_map.104 = (f32[4,2,8,2,8,256]{5,4,3,2,1,0:T(8,128)S(1)}, f32[72,256]{1,0:T(8,128)S(1)}, f32[72,256]{1,0:T(8,128)S(1)}, f32[64,256]{1,0:T(8,128)S(1)}, f32...) custom-call(bf16[4,2,8,2,8,256]{5,4,3,2,1,0:T(8,128)(2,1)S(1)} %copy-done.3, bf16[512,768]{1,0:T(8,128)(2,1)S(1)} %copy-done, ...), custom_call_target="tpu_custom_call" | custom-call | tf_op jit(solution)/shard_map/pallas_call | solution.py:279
  14.8 0.0 copy-start.7
  14.8 4.6 %collective-permute-start = (f32[72,256]{1,0:T(8,128)S(1)}, f32[72,256]{1,0:T(8,128)S(1)}, u32[]{:S(2)}, u32[]{:S(2)}) collective-permute-start(f32[72,256]{1,0:T(8,128)S(1)} %get-tuple-element.15), channel_id=1, source_target_pairs={{0,8},{8,16},{16,24},{24,32},{32,40},{40,48},{48,56},{56,64},{64,7... | collective-permute-start | bytes 221192 | tf_op jit(solution)/shard_map/ppermute | solution.py:302
  19.5 9.8 %collective-permute-start.1 = (f32[72,256]{1,0:T(8,128)S(1)}, f32[72,256]{1,0:T(8,128)S(1)}, u32[]{:S(2)}, u32[]{:S(2)}) collective-permute-start(f32[72,256]{1,0:T(8,128)S(1)} %get-tuple-element.16), channel_id=1, source_target_pairs={{0,760},{8,0},{16,8},{24,16},{32,24},{40,32},{48,40},{56,48},{64,5... | collective-permute-start | bytes 221192 | tf_op jit(solution)/shard_map/ppermute | solution.py:302
  29.3 0.0 collective-permute-done.from_low.low_x
  29.3 0.9 %collective-permute-done.1.from_high.high_x = f32[72,256]{1,0:T(8,128)S(1)} collective-permute-done((f32[72,256]{1,0:T(8,128)S(1)}, f32[72,256]{1,0:T(8,128)S(1)}, u32[]{:S(2)}, u32[]{:S(2)}) %collective-permute-start.1) | collective-permute-done | bytes 73760 | tf_op jit(solution)/shard_map/ppermute | solution.py:302
  30.2 1.9 %collective-permute-start.2 = (f32[72,256]{1,0:T(8,128)S(1)}, f32[72,256]{1,0:T(8,128)S(1)}, u32[]{:S(2)}, u32[]{:S(2)}) collective-permute-start(f32[72,256]{1,0:T(8,128)S(1)} %get-tuple-element.20), channel_id=1, source_target_pairs={{0,1},{1,2},{2,3},{3,4},{4,5},{5,6},{6,7},{7,0},{8,9},{9,10},{10,1... | collective-permute-start | bytes 221192 | tf_op jit(solution)/shard_map/ppermute | solution.py:302
  32.2 4.6 %collective-permute-start.3 = (f32[72,256]{1,0:T(8,128)S(1)}, f32[72,256]{1,0:T(8,128)S(1)}, u32[]{:S(2)}, u32[]{:S(2)}) collective-permute-start(f32[72,256]{1,0:T(8,128)S(1)} %get-tuple-element.21), channel_id=1, source_target_pairs={{0,7},{1,0},{2,1},{3,2},{4,3},{5,4},{6,5},{7,6},{8,15},{9,8},{10,9... | collective-permute-start | bytes 221192 | tf_op jit(solution)/shard_map/ppermute | solution.py:302
  36.7 0.0 copy-done.8
  36.8 0.0 copy-done.7
  36.8 0.2 copy.14.sep
  37.0 0.0 collective-permute-done.2.low_y
  37.0 1.2 %collective-permute-done.3.high_y = f32[72,256]{1,0:T(8,128)S(1)} collective-permute-done((f32[72,256]{1,0:T(8,128)S(1)}, f32[72,256]{1,0:T(8,128)S(1)}, u32[]{:S(2)}, u32[]{:S(2)}) %collective-permute-start.3) | collective-permute-done | bytes 73760 | tf_op jit(solution)/shard_map/ppermute | solution.py:302
  38.1 1.5 %shard_map.106 = (f32[4,2,8,2,8,256]{5,4,3,2,1,0:T(8,128)}, f32[8,128]{1,0:T(8,128)S(1)}, f32[2,2,33]{2,1,0:T(2,128)S(1)}) custom-call(f32[4,2,8,2,8,256]{5,4,3,2,1,0:T(8,128)S(1)} %get-tuple-element.14.partial, f32[72,256]{1,0:T(8,128)S(1)} %collective-permute-done.from_low.low_x, f32[72,256]{1,0:T(8,128)S(1)} %collective-permute-done.1.from_high.high_x, ...), custom_call_target="tpu_custom_call" | custom-call | tf_op jit(solution)/shard_map/pallas_call | solution.py:279
  39.6 15.3 %all_to_all.15 = f32[8,8,128]{2,1,0:T(8,128)S(1)} all-to-all(f32[8,8,128]{2,1,0:T(8,128)S(1)} %broadcast_in_dim.9), channel_id=1, replica_groups=mesh['z'=12,'x'=4,'core'=2,'cross'=8] {'x','core'}, dimensions={0} | all-to-all | bytes 65536 | tf_op jit(solution)/shard_map/all_to_all | solution.py:310
  54.9 13.7 %all_to_all.16 = f32[8,8,128]{2,1,0:T(8,128)S(1)} all-to-all(f32[8,8,128]{2,1,0:T(8,128)S(1)} %broadcast_in_dim.10), channel_id=1, replica_groups=mesh['z'=12,'x'=4,'core'=2,'cross'=8] {'cross'}, dimensions={0} | all-to-all | bytes 65536 | tf_op jit(solution)/shard_map/all_to_all | solution.py:310
  68.6 16.4 %all_to_all.17.arrived = f32[12,8,128]{2,1,0:T(8,128)S(1)} all-to-all(f32[12,8,128]{2,1,0:T(8,128)S(1)} %broadcast_in_dim.11), channel_id=1, replica_groups=mesh['z'=12,'x'=4,'core'=2,'cross'=8] {'z'}, dimensions={0} | all-to-all | bytes 98304 | tf_op jit(solution)/shard_map/all_to_all | solution.py:310
  85.0 0.8 shard_map.107
  (7 shorter events, 0.1 us)
Async XLA Ops:
  0.6 1.1 %copy-start = (bf16[512,768]{1,0:T(8,128)(2,1)S(1)}, bf16[512,768]{1,0:T(8,128)(2,1)}, u32[]{:S(2)}) copy-start(bf16[512,768]{1,0:T(8,128)(2,1)} %constant.14.clone.spread) | copy-start | bytes 2359300
  1.8 1.1 %copy-start.1 = (bf16[3,768,128]{2,1,0:T(8,128)(2,1)S(1)}, bf16[3,768,128]{2,1,0:T(8,128)(2,1)}, u32[]{:S(2)}) copy-start(bf16[3,768,128]{2,1,0:T(8,128)(2,1)} %constant.19.clone.rise) | copy-start | bytes 1769476
  2.8 1.1 %copy-start.2 = (bf16[1152,256]{1,0:T(8,128)(2,1)S(1)}, bf16[1152,256]{1,0:T(8,128)(2,1)}, u32[]{:S(2)}) copy-start(bf16[1152,256]{1,0:T(8,128)(2,1)} %constant.17.clone.gather) | copy-start | bytes 1769476
  3.9 1.0 %copy-start.3 = (bf16[4,2,8,2,8,256]{5,4,3,2,1,0:T(8,128)(2,1)S(1)}, bf16[4,2,8,2,8,256]{5,4,3,2,1,0:T(8,128)(2,1)}, u32[]{:S(2)}) copy-start(bf16[4,2,8,2,8,256]{5,4,3,2,1,0:T(8,128)(2,1)} %fields.1) | copy-start | bytes 1572868
  4.9 1.0 %copy-start.4 = (bf16[3,40,1280]{2,1,0:T(8,128)(2,1)S(1)}, bf16[3,40,1280]{2,1,0:T(8,128)(2,1)}, u32[]{:S(2)}) copy-start(bf16[3,40,1280]{2,1,0:T(8,128)(2,1)} %constant.18.clone.own) | copy-start | bytes 921604
  5.9 0.9 %copy-start.5 = (bf16[432,256]{1,0:T(8,128)(2,1)S(1)}, bf16[432,256]{1,0:T(8,128)(2,1)}, u32[]{:S(2)}) copy-start(bf16[432,256]{1,0:T(8,128)(2,1)} %constant.15.clone.lift) | copy-start | bytes 663556
  6.8 0.8 copy-start.6
  7.7 29.1 %copy-start.8 = (f32[2,2,33,132]{3,1,2,0:T(2,128)S(1)}, f32[2,2,33,132]{3,1,2,0:T(2,128)}, u32[]{:S(2)}) copy-start(f32[2,2,33,132]{3,1,2,0:T(2,128)} %param.11) | copy-start | bytes 209092
  14.8 22.0 %copy-start.7 = (f32[2,2,33,1024]{3,1,2,0:T(2,128)S(1)}, f32[2,2,33,1024]{3,1,2,0:T(2,128)}, u32[]{:S(2)}) copy-start(f32[2,2,33,1024]{3,1,2,0:T(2,128)} %param.10) | copy-start | bytes 1622020
  14.8 14.5 %collective-permute-start = (f32[72,256]{1,0:T(8,128)S(1)}, f32[72,256]{1,0:T(8,128)S(1)}, u32[]{:S(2)}, u32[]{:S(2)}) collective-permute-start(f32[72,256]{1,0:T(8,128)S(1)} %get-tuple-element.15), channel_id=1, source_target_pairs={{0,8},{8,16},{16,24},{24,32},{32,40},{40,48},{48,56},{56,64},{64,7... | collective-permute-start | bytes 221192 | tf_op jit(solution)/shard_map/ppermute | solution.py:302
  19.5 10.7 %collective-permute-start.1 = (f32[72,256]{1,0:T(8,128)S(1)}, f32[72,256]{1,0:T(8,128)S(1)}, u32[]{:S(2)}, u32[]{:S(2)}) collective-permute-start(f32[72,256]{1,0:T(8,128)S(1)} %get-tuple-element.16), channel_id=1, source_target_pairs={{0,760},{8,0},{16,8},{24,16},{32,24},{40,32},{48,40},{56,48},{64,5... | collective-permute-start | bytes 221192 | tf_op jit(solution)/shard_map/ppermute | solution.py:302
  30.2 6.7 %collective-permute-start.2 = (f32[72,256]{1,0:T(8,128)S(1)}, f32[72,256]{1,0:T(8,128)S(1)}, u32[]{:S(2)}, u32[]{:S(2)}) collective-permute-start(f32[72,256]{1,0:T(8,128)S(1)} %get-tuple-element.20), channel_id=1, source_target_pairs={{0,1},{1,2},{2,3},{3,4},{4,5},{5,6},{6,7},{7,0},{8,9},{9,10},{10,1... | collective-permute-start | bytes 221192 | tf_op jit(solution)/shard_map/ppermute | solution.py:302
  32.2 6.0 %collective-permute-start.3 = (f32[72,256]{1,0:T(8,128)S(1)}, f32[72,256]{1,0:T(8,128)S(1)}, u32[]{:S(2)}, u32[]{:S(2)}) collective-permute-start(f32[72,256]{1,0:T(8,128)S(1)} %get-tuple-element.21), channel_id=1, source_target_pairs={{0,7},{1,0},{2,1},{3,2},{4,3},{5,4},{6,5},{7,6},{8,15},{9,8},{10,9... | collective-permute-start | bytes 221192 | tf_op jit(solution)/shard_map/ppermute | solution.py:302
where the time goes:
time: 87.6 us; the launch traced here: 85.9 us
  blocking collectives  45.4 us (52%)
  starting transfers between devices  21 us (24%)
  Pallas kernels  9.48 us (11%)
  local copies, waits for them, and re-layouts  7.25 us (8%)
  waiting for transfers between devices  2.04 us (2%)
    all_to_all x3, blocking collectives, scattered(): lax.all_to_all(jnp.broadcast_to(tile, (count,) + tile.shape), axis, 0, 0)  45.4 us
    ppermute x4, starting transfers between devices, shifted(): return lax.ppermute(x, axis, [(i, (i + by) % count) for i in range(count)])  21 us
    pallas_call x4, Pallas kernels, call(): pl.pallas_call(kernel, out_shape=[jax.ShapeDtypeStruct(s, f32) for s in s...  9.48 us
    unnamed x20, local copies, waits for them, and re-layouts  7.24 us
    ppermute x4, waiting for transfers between devices, shifted(): return lax.ppermute(x, axis, [(i, (i + by) % count) for i in range(count)])  2.04 us
  transfers between devices with their start and end apart: 4, of which 2 were waited for; matrix products, arithmetic and copies ran while one was open for 0% of the time, Pallas kernels for 0%

commit v1 on v0

v1 whole, which is shorter than its diff:
```python
import functools

import jax
import jax.numpy as jnp
import numpy as np
from jax import lax
from jax.experimental import pallas as pl
from jax.experimental.pallas import tpu as pltpu
from jax.sharding import Mesh
from jax.sharding import PartitionSpec as P

degree = 7
step_size = 0.25
bf16 = jnp.bfloat16
f32 = jnp.float32


def legendre_values(order, points):
    earlier = points * 0.0 + 1.0
    current = points * 1.0
    for level_index in range(1, order):
        follow = ((2 * level_index + 1) * points * current - level_index * earlier) / (
            level_index + 1
        )
        earlier = current
        current = follow
    return current


def tables():
    gll_nodes = np.array(
        [
            -1.0,
            -0.8717401485096066,
            -0.5917001814331423,
            -0.2092992179024789,
            0.2092992179024789,
            0.5917001814331423,
            0.8717401485096066,
            1.0,
        ]
    )
    at_nodes = legendre_values(degree, gll_nodes)
    weights = 2.0 / (degree * (degree + 1) * at_nodes**2)
    points = degree + 1
    derivative = np.zeros((points, points))
    for target in range(points):
        for source in range(points):
            if target != source:
                derivative[target, source] = at_nodes[target] / (
                    at_nodes[source] * (gll_nodes[target] - gll_nodes[source])
                )
    derivative[0, 0] = -degree * (degree + 1) / 4.0
    derivative[-1, -1] = degree * (degree + 1) / 4.0
    half_nodes = np.array(
        [
            0.1252334085114689,
            0.3678314989981802,
            0.5873179542866175,
            0.7699026741943047,
            0.9041172563704749,
            0.9815606342467192,
        ]
    )
    fine_nodes = np.concatenate([-half_nodes[::-1], half_nodes])
    for newton_step in range(3):
        top_value = legendre_values(12, fine_nodes)
        below_value = legendre_values(11, fine_nodes)
        slope_value = (
            12.0 * (fine_nodes * top_value - below_value) / (fine_nodes * fine_nodes - 1.0)
        )
        fine_nodes = fine_nodes - top_value / slope_value
    top_value = legendre_values(12, fine_nodes)
    below_value = legendre_values(11, fine_nodes)
    slope_value = 12.0 * (fine_nodes * top_value - below_value) / (fine_nodes * fine_nodes - 1.0)
    fine_weights = 2.0 / ((1.0 - fine_nodes * fine_nodes) * slope_value * slope_value)
    interp = np.ones((12, points))
    for source in range(points):
        for target in range(points):
            if target != source:
                interp[:, source] *= (fine_nodes - gll_nodes[target]) / (
                    gll_nodes[source] - gll_nodes[target]
                )
    slope_interp = interp @ derivative
    vertex_hats = np.stack([(1.0 - gll_nodes) / 2.0, (1.0 + gll_nodes) / 2.0]) * weights[None, :]
    return weights, derivative, interp, slope_interp, fine_weights, vertex_hats


def halves(matrix):
    high = matrix.astype(np.float32).astype(jnp.bfloat16)
    low = (matrix - high.astype(np.float64)).astype(np.float32).astype(jnp.bfloat16)
    return high, low


def split(x):
    high = x.astype(bf16)
    return high, (x - high.astype(f32)).astype(bf16)


def constants(ez):
    weights, derivative, interp, slope_interp, fine_weights, hats = tables()
    eye = np.eye(ez)
    flat, steep = np.kron(eye, interp.T), np.kron(eye, slope_interp.T)
    spread = []
    for at, rows in ((0, slice(0, 128)), (2, slice(128, 256)), (1, slice(0, 256))):
        lanes = slice(128 * at, 128 * at + 128)
        spread += halves(np.concatenate([flat[rows, lanes], steep[rows, lanes]], axis=1))
    spread = np.concatenate(spread, axis=0)
    lift = np.concatenate(
        [np.kron(interp, interp), np.kron(slope_interp, interp), np.kron(interp, slope_interp)]
    )
    high, low = halves(lift)
    lift = np.concatenate([high, low, high, low], axis=1)
    across = weights.copy()
    across[0] = across[7] = weights[0] + weights[7]
    back = interp.T * fine_weights[None, :]
    fall = -np.kron(back / across[:, None], back / across[:, None])
    high, low = halves(fall)
    fall = np.concatenate([high, high, low], axis=1)
    joined = np.eye(8 * ez)
    for at in range(ez - 1):
        joined[8 * at + 7, 8 * at + 8] = joined[8 * at + 8, 8 * at + 7] = 1.0
    mass = joined @ np.tile(weights, ez)
    gather = np.kron(eye, back.T) @ joined / mass[None, :]
    sides = []
    for at in (0, 128):
        high, low = halves(gather[at : at + 256, at : at + 128])
        sides.append(np.concatenate([high, high, low], axis=0))
    gather = np.stack(sides)
    own, rise = [], []
    slope_hats = hats @ derivative
    for f in range(3):
        own_pair, wide_pair = [], []
        for d in range(2):
            hat = slope_hats if f == d else hats
            rows = 8 if d else 5
            plain = np.zeros((rows, 16))
            for e in range(2):
                for a in range(2):
                    plain[e + a + 1, 8 * e : 8 * e + 8] += hat[a]
            shared = plain.copy()
            for a in range(2):
                shared[a, 0] += hat[a, 7]
                shared[3 + a, 15] += hat[a, 0]
            own_pair.append(plain)
            wide_pair.append(shared)
        own_high, own_low = halves(np.kron(*own_pair))
        wide_high, wide_low = halves(step_size * np.kron(*wide_pair))
        own.append(np.concatenate([own_high, own_low, wide_high, wide_high, wide_low], axis=1))
        hat = slope_hats if f == 2 else hats
        up = np.zeros((8 * ez, 128))
        for e in range(ez):
            for a in range(2):
                up[8 * e : 8 * e + 8, e + a] += hat[a]
        high, low = halves(up)
        rise.append(np.concatenate([high, high, low], axis=0))
    fall = np.pad(fall.astype(np.float32), ((0, 0), (0, 80))).astype(jnp.bfloat16)
    blocks = [spread, lift, fall[:, :256], fall[:, 256:], np.concatenate(list(gather), axis=1)]
    blocks += [np.pad(own[f][:, 256 * c : 256 * c + 256].astype(np.float32), ((0, 8), (0, 0))).astype(jnp.bfloat16)
               for f in range(3) for c in range(5)]
    blocks += [np.concatenate(rise[:2], axis=1), np.concatenate([rise[2], rise[2]], axis=1)]
    return np.concatenate(blocks, axis=0)


def first_kernel(
    fields_far, table_far, out_far, near_side, far_side, low_y, high_y, hold,
    fields, table, points, down, out, arrivals, departure,
):
    ends = (0, 1024, 1584, 2352, 4608)
    loads = [pltpu.make_async_copy(fields_far, fields, arrivals.at[0])]
    for at in range(4):
        rows = pl.ds(ends[at], ends[at + 1] - ends[at])
        loads.append(
            pltpu.make_async_copy(table_far.at[rows], table.at[rows], arrivals.at[at + 1])
        )
    for load in loads:
        load.start()
    loads[0].wait()
    nodes = fields[...].astype(f32).reshape(1024, 256).astype(bf16)
    loads[1].wait()
    for at, piece, rows in (
        (0, nodes[:, :128], slice(0, 256)),
        (512, nodes[:, 128:], slice(256, 512)),
        (256, nodes, slice(512, 1024)),
    ):
        points[..., at : at + 256] = jnp.dot(
            jnp.concatenate([piece, piece], axis=1), table[rows], preferred_element_type=f32
        ).reshape(4, 2, 8, 2, 8, 256)
    loads[2].wait()

    def column(ex, carry):
        lift = table[1024:1456]
        fall = jnp.concatenate([table[1456:1520], table[1520:1584][:, :176]], axis=1)
        speeds = []
        slopes = []
        for f in range(4):
            first = points[f, ex, :, 0].reshape(64, 768)
            second = points[f, ex, :, 1].reshape(64, 768)
            sides = []
            for side in range(2):
                lanes = [slice(at, at + 128) for at in range(128 * side, 768, 256)]
                pieces = [first[:, at] for at in lanes] + [second[:, at] for at in lanes]
                high, low = split(jnp.concatenate(pieces, axis=1))
                sides.append(jnp.concatenate([high, high, low, low], axis=0))
            flat = jnp.dot(lift, sides[0], preferred_element_type=f32)
            steep = jnp.dot(lift[:144], sides[1], preferred_element_type=f32)
            if f < 3:
                speeds.append(flat[:144])
            slopes.append((flat[144:288], flat[288:], steep))
        for f in range(4):
            product = sum(speeds[d] * slopes[f][d] for d in range(3))
            high, low = split(product)
            stacked = jnp.concatenate([high, low, high], axis=0)
            fallen = jnp.dot(fall, stacked, preferred_element_type=f32)
            down[f, ex, :, 0] = fallen[:, :384].reshape(8, 8, 384)
            down[f, ex, :, 1] = fallen[:, 384:].reshape(8, 8, 384)
        return carry

    lax.fori_loop(0, 2, column, 0)
    high, low = split(down[...].reshape(1024, 384))
    loads[3].wait()
    for at in (0, 128):
        lanes = slice(at, at + 256)
        stacked = jnp.concatenate([high[:, lanes], low[:, lanes], high[:, lanes]], axis=1)
        out[..., at : at + 128] = jnp.dot(
            stacked, table[1584:2352, at : at + 128], preferred_element_type=f32
        ).reshape(4, 2, 8, 2, 8, 128)
    middle = out[:, 0, 7] + out[:, 1, 0]
    out[:, 0, 7] = middle
    out[:, 1, 0] = middle
    middle = out[:, :, :, 0, 7:8] + out[:, :, :, 1, 0:1]
    out[:, :, :, 0, 7:8] = middle
    out[:, :, :, 1, 0:1] = middle
    store = pltpu.make_async_copy(out, out_far, departure)
    store.start()
    low_y[...] = out[:, :, :, 0, 0].reshape(64, 256)
    high_y[...] = out[:, :, :, 1, 7].reshape(64, 256)
    loads[4].wait()
    total = jnp.zeros((40, 128), f32)
    for f in range(3):
        high, low = split(out[f].reshape(256, 256))
        part = nodes[256 * f : 256 * (f + 1)]
        stacked = jnp.concatenate([part, part, high, low, high], axis=0)
        own = [table[2352 + 48 * c : 2400 + 48 * c] for c in range(5 * f, 5 * f + 5)]
        flat = jnp.dot(jnp.concatenate(own, axis=1), stacked, preferred_element_type=f32)
        high, low = split(flat[:40])
        start, lanes = 3072 + 768 * (f // 2), slice(128 * (f % 2), 128 * (f % 2) + 128)
        total = total + jnp.dot(
            jnp.concatenate([high, low, high], axis=1),
            table[start : start + 768, lanes],
            preferred_element_type=f32,
        )
    hold[...] = total[8:24]
    even = lax.axis_index("core") == 0
    low_face = out[:, 0, 0].reshape(64, 256)
    high_face = out[:, 1, 7].reshape(64, 256)
    far_side[:64] = jnp.where(even, low_face, high_face)
    far_side[64:, :128] = jnp.where(even, total[:8], total[24:32])
    far_side[64:, 128:] = jnp.where(even, 0.0, total[32:])
    chosen = jnp.where(even, high_face, low_face)
    first = jnp.where(even, total[24:32], total[:8])
    second = jnp.where(even, total[32:], 0.0)
    near_side[:64] = chosen
    near_side[64:, :128] = first
    near_side[64:, 128:] = second
    store.wait()


def sides(near_side, far_side, axis):
    me = lax.axis_index(axis)
    even = me == 0
    beside = near_side[1 - me]
    beyond = far_side[...]
    return jnp.where(even, beyond, beside), jnp.where(even, beside, beyond)


def second_kernel(
    near_side, far_side, low_y, high_y, hold, near_out, far_out, hold_out, from_low, from_high
):
    from_low[...], from_high[...] = sides(near_side, far_side, "core")
    even = lax.axis_index("pair") == 0
    low_face = low_y[...]
    high_face = high_y[...]
    near_out[:64] = jnp.where(even, high_face, low_face)
    far_out[:64] = jnp.where(even, low_face, high_face)
    for f in range(4):
        for at, source, row in ((16 * f, from_low, 16 * f), (16 * f + 15, from_high, 16 * f)):
            place = slice(at, at + 1)
            low_sum = low_y[place] + source[row : row + 1]
            high_sum = high_y[place] + source[row + 15 : row + 16]
            near_out[place] = jnp.where(even, high_sum, low_sum)
            far_out[place] = jnp.where(even, low_sum, high_sum)
    near = hold[:8] + from_low[64:, :128]
    far = hold[8:] + from_low[64:, 128:] + from_high[64:, :128]
    hold_out[:8] = near
    hold_out[8:] = far
    for target in (near_out, far_out):
        target[64:, :128] = near
        target[64:, 128:] = far


def third_kernel(partial, from_low, from_high, out):
    out[...] = partial[...]
    out[:, 0, 0] = partial[:, 0, 0] + from_low[:64].reshape(4, 2, 8, 256)
    out[:, 1, 7] = partial[:, 1, 7] + from_high[:64].reshape(4, 2, 8, 256)


def fourth_kernel(near_side, far_side, hold, sep, inner, sums, term):
    low_rows, high_rows = sides(near_side.at[:, 64:], far_side.at[64:], "pair")
    rows = []
    for vx in range(2):
        lanes = slice(128 * vx, 128 * vx + 128)
        rows.append(hold[8 * vx + 1 : 8 * vx + 2] + low_rows[3:4, lanes])
        rows.append(
            hold[8 * vx + 2 : 8 * vx + 3] + low_rows[4:5, lanes] + high_rows[0:1, lanes]
        )
    upright = jnp.transpose(jnp.concatenate(rows + rows, axis=0))
    columns = [upright[:33, v : v + 1] for v in range(4)]
    for at in range(8):
        lanes = slice(128 * at, 128 * at + 128)
        total = sum(columns[v] * sep[v // 2, v % 2, :, lanes] for v in range(4))
        sums[at : at + 1] = jnp.sum(total, axis=0, keepdims=True)
    total = sum(columns[v] * inner[v // 2, v % 2] for v in range(4))
    total = jnp.sum(total, axis=0, keepdims=True)
    for v in range(4):
        term[v // 2, v % 2 : v % 2 + 1] = lax.dot_general(
            total, inner[v // 2, v % 2], (((1,), (1,)), ((), ())),
            precision=lax.Precision.HIGHEST, preferred_element_type=f32,
        )


def fifth_kernel(partial, near_side, far_side, out):
    low_face, high_face = sides(near_side.at[:, :64], far_side.at[:64], "pair")
    out[...] = partial[...]
    out[:, :, :, 0, 0] = partial[:, :, :, 0, 0] + low_face.reshape(4, 2, 8, 256)
    out[:, :, :, 1, 7] = partial[:, :, :, 1, 7] + high_face.reshape(4, 2, 8, 256)


def spread_kernel(parts, copies):
    total = jnp.sum(parts[...], axis=0)
    copies[...] = jnp.broadcast_to(total[None], copies.shape)


def last_kernel(arrived, sep, term, out):
    total = jnp.sum(arrived[...], axis=0)
    ones = jnp.ones((1, 128), f32)
    for v in range(4):
        spread_out = sum(
            sep[v // 2, v % 2, :, 128 * at : 128 * at + 128] * total[at : at + 1] for at in range(8)
        )
        out[v // 2, v % 2 : v % 2 + 1] = term[v // 2, v % 2 : v % 2 + 1] + lax.dot_general(
            ones, spread_out, (((1,), (1,)), ((), ())),
            precision=lax.Precision.HIGHEST, preferred_element_type=f32,
        )


def call(kernel, shapes, arrays):
    whole = pl.BlockSpec(memory_space=pltpu.VMEM)
    return pl.pallas_call(
        kernel,
        out_shape=[jax.ShapeDtypeStruct(s, f32) for s in shapes],
        in_specs=[whole] * len(arrays),
        out_specs=[whole] * len(shapes),
        compiler_params=pltpu.CompilerParams(vmem_limit_bytes=16 * 2**20),
    )(*arrays)


def first(fields):
    arrays = [fields, jnp.asarray(constants(fields.shape[5] // 8))]
    shapes = [fields.shape, (72, 256), (72, 256), (64, 256), (64, 256), (16, 128)]
    whole = pl.BlockSpec(memory_space=pltpu.VMEM)
    beyond = pl.BlockSpec(memory_space=pltpu.HBM)
    return pl.pallas_call(
        first_kernel,
        out_shape=[jax.ShapeDtypeStruct(s, f32) for s in shapes],
        in_specs=[beyond, beyond],
        out_specs=[beyond] + [whole] * 5,
        scratch_shapes=[pltpu.VMEM(a.shape, a.dtype) for a in arrays]
        + [
            pltpu.VMEM((4, 2, 8, 2, 8, 768), f32),
            pltpu.VMEM((4, 2, 8, 2, 8, 384), f32),
            pltpu.VMEM(fields.shape, f32),
            pltpu.SemaphoreType.DMA((5,)),
            pltpu.SemaphoreType.DMA,
        ],
        compiler_params=pltpu.CompilerParams(vmem_limit_bytes=214 * 2**18),
    )(*arrays)


def moved(x, axis, target):
    return lax.ppermute(x, axis, [(i, target(i)) for i in range(lax.axis_size(axis))])


slab = ("z", "x", "core")
cross = ("half", "pair")


def swapped(x, axis):
    count = lax.axis_size(axis)
    return moved(x, axis, lambda i: (i + (1 if i % 2 else count - 1)) % count)


def scattered(parts, axis):
    copies = call(spread_kernel, [(lax.axis_size(axis),) + parts.shape[1:]], [parts])[0]
    return lax.all_to_all(copies, axis, 0, 0)


def local(fields, sep_factor, local_factor):
    partial, near_side, far_side, low_y, high_y, hold = first(fields)
    far_side = swapped(far_side, slab)
    near_side = lax.all_gather(near_side, "core")
    near_y, far_y, hold, from_low, from_high = call(
        second_kernel,
        [(72, 256), (72, 256), (16, 128), (72, 256), (72, 256)],
        [near_side, far_side, low_y, high_y, hold],
    )
    far_y = swapped(far_y, cross)
    near_y = lax.all_gather(near_y, "pair")
    partial = call(third_kernel, [fields.shape], [partial, from_low, from_high])[0]
    sums, term = call(
        fourth_kernel, [(8, 128), (2, 2, 33)], [near_y, far_y, hold, sep_factor, local_factor]
    )
    conv_rate = call(fifth_kernel, [fields.shape], [partial, near_y, far_y])[0]
    sums = lax.all_gather(sums, "core")
    sums = scattered(sums, ("x",) + cross)
    sums = scattered(sums, "z")
    pressure = call(last_kernel, [(2, 2, 33)], [sums, sep_factor, term])[0]
    return conv_rate, pressure


def solution(mesh):
    fine = Mesh(mesh.devices.reshape(12, 4, 2, 4, 2), slab + cross)
    return jax.shard_map(
        local,
        mesh=fine,
        in_specs=(
            P(None, slab, None, cross, None, None),
            P(slab, cross, None, None),
            P(slab, cross, None, None),
        ),
        out_specs=(P(None, slab, None, cross, None, None), P(slab, cross, None)),
        check_vma=False,
    )
```

time: 87.6 us -> 73.3 us (0.84)
  the two profiles are of different devices: /device:TPU:1 before, /device:TPU:8 now
where the time goes in v1:
time: 73.3 us; the launch traced here: 73 us
  starting transfers between devices  26.1 us (36%)
  blocking collectives  25.3 us (35%)
  Pallas kernels  10.9 us (15%)
  waiting for transfers between devices  9.71 us (13%)
  between operations  0.74 us (1%)
    ppermute x2, starting transfers between devices, moved(): lax.ppermute(x, axis, [(i, target(i)) for i in range(lax.axis_size(axis))])  19.8 us
    all_to_all x1, blocking collectives, scattered(): return lax.all_to_all(copies, axis, 0, 0)  16.3 us
    all_to_all x1, waiting for transfers between devices, scattered(): return lax.all_to_all(copies, axis, 0, 0)  9.6 us
    pallas_call x1, Pallas kernels, first(): pl.pallas_call(first_kernel, out_shape=[jax.ShapeDtypeStruct(s, f32) for...  7.71 us
    all_to_all x1, starting transfers between devices, scattered(): return lax.all_to_all(copies, axis, 0, 0)  6.29 us
    all_gather x1, blocking collectives, local(): near_y = lax.all_gather(near_y, 'pair')  5.33 us
    pallas_call x7, Pallas kernels, call(): pl.pallas_call(kernel, out_shape=[jax.ShapeDtypeStruct(s, f32) for s in s...  3.21 us
    all_gather x1, blocking collectives, local(): near_side = lax.all_gather(near_side, 'core')  1.91 us
  transfers between devices with their start and end apart: 3, of which 2 were waited for; matrix products, arithmetic and copies ran while one was open for 0% of the time, Pallas kernels for 2%

profile of v1, /device:TPU:8, one launch (start us, length us, event | category | flops | bytes accessed | tf_op | source)
XLA Modules:
  0.0 73.0 jit_solution(7181992151881496481)
XLA Ops:
  0.6 0.0 copy-start.1
  0.6 0.0 copy-start.2
  0.6 7.7 %shard_map.59 = (f32[4,2,8,2,8,256]{5,4,3,2,1,0:T(8,128)}, f32[72,256]{1,0:T(8,128)S(1)}, f32[72,256]{1,0:T(8,128)S(1)}, f32[64,256]{1,0:T(8,128)S(1)}, f32[64,256]{1,0:T(8,128)S(1)}, /*index=5*/f32[16,128]{1,0:T(8,128)S(1)}) custom-call(bf16[4,2,8,2,8,256]{5,4,3,2,1,0:T(8,128)(2,1)} %fields_far.1, bf16[4608,256]{1,0:T(8,128)(2,1)} %constant.2.clone.table_far), custom_call_target="tpu_custom_call" | custom-call | tf_op jit(solution)/shard_map/pallas_call | solution.py:373
  8.4 0.0 copy-start
  8.4 16.4 %collective-permute-start = (f32[72,256]{1,0:T(8,128)S(1)}, f32[72,256]{1,0:T(8,128)S(1)}, u32[]{:S(2)}, u32[]{:S(2)}) collective-permute-start(f32[72,256]{1,0:T(8,128)S(1)} %get-tuple-element.17), channel_id=1, source_target_pairs={{0,760},{8,16},{16,8},{24,32},{32,24},{40,48},{48,40},{56,64},{64,... | collective-permute-start | bytes 221192 | tf_op jit(solution)/shard_map/ppermute | solution.py:391
  24.7 1.9 %all-gather = f32[144,256]{1,0:T(8,128)S(1)} all-gather(f32[72,256]{1,0:T(8,128)S(1)} %get-tuple-element.16), channel_id=2, replica_groups=mesh['z'=12,'x'=4,'core'=2,'half'=4,'pair'=2] {'core'}, dimensions={0}, use_global_device_ids=true | all-gather | bytes 221184 | tf_op jit(solution)/shard_map/all_gather | solution.py:411
  26.6 0.1 collective-permute-done.far_side
  26.8 3.5 %collective-permute-start.1 = (f32[72,256]{1,0:T(8,128)S(1)}, f32[72,256]{1,0:T(8,128)S(1)}, u32[]{:S(2)}, u32[]{:S(2)}) collective-permute-start(f32[72,256]{1,0:T(8,128)S(1)} %get-tuple-element.24), channel_id=1, source_target_pairs={{0,7},{1,2},{2,1},{3,4},{4,3},{5,6},{6,5},{7,0},{8,15},{9,10},{10,... | collective-permute-start | bytes 221192 | tf_op jit(solution)/shard_map/ppermute | solution.py:391
  30.3 0.0 copy-done.1
  30.3 0.2 copy.6.sep
  30.5 0.0 copy-done.2
  30.5 5.3 %all-gather.1 = f32[144,256]{1,0:T(8,128)S(1)} all-gather(f32[72,256]{1,0:T(8,128)S(1)} %get-tuple-element.23), channel_id=3, replica_groups=mesh['z'=12,'x'=4,'core'=2,'half'=4,'pair'=2] {'pair'}, dimensions={0}, use_global_device_ids=true | all-gather | bytes 221184 | tf_op jit(solution)/shard_map/all_gather | solution.py:418
  35.8 0.0 collective-permute-done.1.far_side
  35.9 0.4 shard_map.63
  36.3 1.8 %all-gather.2 = f32[16,128]{1,0:T(8,128)S(1)} all-gather(f32[8,128]{1,0:T(8,128)S(1)} %get-tuple-element.26), channel_id=4, replica_groups=mesh['z'=12,'x'=4,'core'=2,'half'=4,'pair'=2] {'core'}, dimensions={0}, use_global_device_ids=true | all-gather | bytes 12288 | tf_op jit(solution)/shard_map/all_gather | solution.py:424
  38.1 16.3 %all_to_all.10.parts = f32[32,8,128]{2,1,0:T(8,128)S(1)} all-to-all(f32[32,8,128]{2,1,0:T(8,128)S(1)} %shard_map.64), channel_id=1, replica_groups=mesh['z'=12,'x'=4,'core'=2,'half'=4,'pair'=2] {'x','half','pair'}, dimensions={0} | all-to-all | bytes 262144 | tf_op jit(solution)/shard_map/all_to_all | solution.py:405
  54.4 0.7 shard_map.65
  55.0 6.3 %all-to-all-start.1 = ((f32[12,8,128]{2,1,0:T(8,128)}), f32[12,8,128]{2,1,0:T(8,128)S(1)}, u32[]{:S(2)}, u32[]{:S(2)}) async-start(f32[12,8,128]{2,1,0:T(8,128)} %shard_map.65), calls=%async_computation.1 | async-start | bytes 98304 | tf_op jit(solution)/shard_map/all_to_all | solution.py:405
  61.3 0.0 copy-done
  61.3 0.1 shard_map.61.partial
  61.4 1.1 %shard_map.62 = f32[4,2,8,2,8,256]{5,4,3,2,1,0:T(8,128)} custom-call(f32[4,2,8,2,8,256]{5,4,3,2,1,0:T(8,128)S(1)} %shard_map.61.partial, f32[2,72,256]{2,1,0:T(8,128)S(1)} %bitcast.4, f32[72,256]{1,0:T(8,128)S(1)} %collective-permute-done.1.far_side), custom_call_target="tpu_custom_call" | custom-call | tf_op jit(solution)/shard_map/pallas_call | solution.py:359
  62.6 9.6 %all-to-all-done.1.arrived = f32[12,8,128]{2,1,0:T(8,128)S(1)} async-done(((f32[12,8,128]{2,1,0:T(8,128)}), f32[12,8,128]{2,1,0:T(8,128)S(1)}, u32[]{:S(2)}, u32[]{:S(2)}) %all-to-all-start.1) | async-done | bytes 49184 | tf_op jit(solution)/shard_map/all_to_all | solution.py:405
  72.2 0.8 %shard_map.66 = f32[2,2,33]{2,1,0:T(2,128)} custom-call(f32[12,8,128]{2,1,0:T(8,128)S(1)} %all-to-all-done.1.arrived, f32[2,2,33,1024]{3,2,1,0:T(8,128)S(1)} %copy.6.sep, f32[2,2,33]{2,1,0:T(2,128)S(1)} %get-tuple-element.27.term), custom_call_target="tpu_custom_call" | custom-call | tf_op jit(solution)/shard_map/pallas_call | solution.py:359
  (3 shorter events, 0.1 us)
Async XLA Ops:
  0.6 29.7 %copy-start.1 = (f32[2,2,33,1024]{3,1,2,0:T(2,128)S(1)}, f32[2,2,33,1024]{3,1,2,0:T(2,128)}, u32[]{:S(2)}) copy-start(f32[2,2,33,1024]{3,1,2,0:T(2,128)} %param.5) | copy-start | bytes 1622020
  0.6 29.8 %copy-start.2 = (f32[2,2,33,132]{3,1,2,0:T(2,128)S(1)}, f32[2,2,33,132]{3,1,2,0:T(2,128)}, u32[]{:S(2)}) copy-start(f32[2,2,33,132]{3,1,2,0:T(2,128)} %param.6) | copy-start | bytes 209092
  8.4 53.0 %copy-start = (f32[4,2,8,2,8,256]{5,4,3,2,1,0:T(8,128)S(1)}, f32[4,2,8,2,8,256]{5,4,3,2,1,0:T(8,128)}, u32[]{:S(2)}) copy-start(f32[4,2,8,2,8,256]{5,4,3,2,1,0:T(8,128)} %get-tuple-element.15.partial) | copy-start | bytes 3145732
  8.4 18.4 %collective-permute-start = (f32[72,256]{1,0:T(8,128)S(1)}, f32[72,256]{1,0:T(8,128)S(1)}, u32[]{:S(2)}, u32[]{:S(2)}) collective-permute-start(f32[72,256]{1,0:T(8,128)S(1)} %get-tuple-element.17), channel_id=1, source_target_pairs={{0,760},{8,16},{16,8},{24,32},{32,24},{40,48},{48,40},{56,64},{64,... | collective-permute-start | bytes 221192 | tf_op jit(solution)/shard_map/ppermute | solution.py:391
  26.8 9.1 %collective-permute-start.1 = (f32[72,256]{1,0:T(8,128)S(1)}, f32[72,256]{1,0:T(8,128)S(1)}, u32[]{:S(2)}, u32[]{:S(2)}) collective-permute-start(f32[72,256]{1,0:T(8,128)S(1)} %get-tuple-element.24), channel_id=1, source_target_pairs={{0,7},{1,2},{2,1},{3,4},{4,3},{5,6},{6,5},{7,0},{8,15},{9,10},{10,... | collective-permute-start | bytes 221192 | tf_op jit(solution)/shard_map/ppermute | solution.py:391
  55.0 17.1 %all-to-all-start.1 = ((f32[12,8,128]{2,1,0:T(8,128)}), f32[12,8,128]{2,1,0:T(8,128)S(1)}, u32[]{:S(2)}, u32[]{:S(2)}) async-start(f32[12,8,128]{2,1,0:T(8,128)} %shard_map.65), calls=%async_computation.1 | async-start | bytes 98304 | tf_op jit(solution)/shard_map/all_to_all | solution.py:405

commit v2 on v1

--- a/solution.py
+++ b/solution.py
@@ -107,7 +107,7 @@
         spread += halves(np.concatenate([flat[rows, lanes], steep[rows, lanes]], axis=1))
     spread = np.concatenate(spread, axis=0)
     lift = np.concatenate(
-        [np.kron(interp, interp), np.kron(slope_interp, interp), np.kron(interp, slope_interp)]
+        [np.kron(slope_interp, interp), np.kron(interp, slope_interp), np.kron(interp, interp)]
     )
     high, low = halves(lift)
     lift = np.concatenate([high, low, high, low], axis=1)
@@ -122,11 +122,8 @@
         joined[8 * at + 7, 8 * at + 8] = joined[8 * at + 8, 8 * at + 7] = 1.0
     mass = joined @ np.tile(weights, ez)
     gather = np.kron(eye, back.T) @ joined / mass[None, :]
-    sides = []
-    for at in (0, 128):
-        high, low = halves(gather[at : at + 256, at : at + 128])
-        sides.append(np.concatenate([high, high, low], axis=0))
-    gather = np.stack(sides)
+    high, low = halves(gather)
+    gather = np.concatenate([high, high, low], axis=0)
     own, rise = [], []
     slope_hats = hats @ derivative
     for f in range(3):
@@ -155,7 +152,7 @@
         high, low = halves(up)
         rise.append(np.concatenate([high, high, low], axis=0))
     fall = np.pad(fall.astype(np.float32), ((0, 0), (0, 80))).astype(jnp.bfloat16)
-    blocks = [spread, lift, fall[:, :256], fall[:, 256:], np.concatenate(list(gather), axis=1)]
+    blocks = [spread, lift, fall[:, :256], fall[:, 256:], gather]
     blocks += [np.pad(own[f][:, 256 * c : 256 * c + 256].astype(np.float32), ((0, 8), (0, 0))).astype(jnp.bfloat16)
                for f in range(3) for c in range(5)]
     blocks += [np.concatenate(rise[:2], axis=1), np.concatenate([rise[2], rise[2]], axis=1)]
@@ -166,7 +163,7 @@
     fields_far, table_far, out_far, near_side, far_side, low_y, high_y, hold,
     fields, table, points, down, out, arrivals, departure,
 ):
-    ends = (0, 1024, 1584, 2352, 4608)
+    ends = (0, 1024, 1584, 2736, 4992)
     loads = [pltpu.make_async_copy(fields_far, fields, arrivals.at[0])]
     for at in range(4):
         rows = pl.ds(ends[at], ends[at + 1] - ends[at])
@@ -202,11 +199,11 @@
                 pieces = [first[:, at] for at in lanes] + [second[:, at] for at in lanes]
                 high, low = split(jnp.concatenate(pieces, axis=1))
                 sides.append(jnp.concatenate([high, high, low, low], axis=0))
-            flat = jnp.dot(lift, sides[0], preferred_element_type=f32)
-            steep = jnp.dot(lift[:144], sides[1], preferred_element_type=f32)
+            flat = jnp.dot(lift if f < 3 else lift[:288], sides[0], preferred_element_type=f32)
+            steep = jnp.dot(lift[288:], sides[1], preferred_element_type=f32)
             if f < 3:
-                speeds.append(flat[:144])
-            slopes.append((flat[144:288], flat[288:], steep))
+                speeds.append(flat[288:])
+            slopes.append((flat[:144], flat[144:288], steep))
         for f in range(4):
             product = sum(speeds[d] * slopes[f][d] for d in range(3))
             high, low = split(product)
@@ -216,23 +213,25 @@
             down[f, ex, :, 1] = fallen[:, 384:].reshape(8, 8, 384)
         return carry
 
-    lax.fori_loop(0, 2, column, 0)
+    column(0, 0)
+    column(1, 0)
     high, low = split(down[...].reshape(1024, 384))
     loads[3].wait()
-    for at in (0, 128):
-        lanes = slice(at, at + 256)
-        stacked = jnp.concatenate([high[:, lanes], low[:, lanes], high[:, lanes]], axis=1)
-        out[..., at : at + 128] = jnp.dot(
-            stacked, table[1584:2352, at : at + 128], preferred_element_type=f32
-        ).reshape(4, 2, 8, 2, 8, 128)
-    middle = out[:, 0, 7] + out[:, 1, 0]
-    out[:, 0, 7] = middle
-    out[:, 1, 0] = middle
-    middle = out[:, :, :, 0, 7:8] + out[:, :, :, 1, 0:1]
-    out[:, :, :, 0, 7:8] = middle
-    out[:, :, :, 1, 0:1] = middle
-    store = pltpu.make_async_copy(out, out_far, departure)
-    store.start()
+    stacked = jnp.concatenate([high, low, high], axis=1)
+    stores = []
+    for pair in range(2):
+        part = pl.ds(2 * pair, 2)
+        out[part] = jnp.dot(
+            stacked[512 * pair : 512 * pair + 512], table[1584:2736], preferred_element_type=f32
+        ).reshape(2, 2, 8, 2, 8, 256)
+        middle = out[part, 0, 7] + out[part, 1, 0]
+        out[part, 0, 7] = middle
+        out[part, 1, 0] = middle
+        middle = out[part, :, :, 0, 7:8] + out[part, :, :, 1, 0:1]
+        out[part, :, :, 0, 7:8] = middle
+        out[part, :, :, 1, 0:1] = middle
+        stores.append(pltpu.make_async_copy(out.at[part], out_far.at[part], departure.at[pair]))
+        stores[pair].start()
     low_y[...] = out[:, :, :, 0, 0].reshape(64, 256)
     high_y[...] = out[:, :, :, 1, 7].reshape(64, 256)
     loads[4].wait()
@@ -241,10 +240,10 @@
         high, low = split(out[f].reshape(256, 256))
         part = nodes[256 * f : 256 * (f + 1)]
         stacked = jnp.concatenate([part, part, high, low, high], axis=0)
-        own = [table[2352 + 48 * c : 2400 + 48 * c] for c in range(5 * f, 5 * f + 5)]
+        own = [table[2736 + 48 * c : 2784 + 48 * c] for c in range(5 * f, 5 * f + 5)]
         flat = jnp.dot(jnp.concatenate(own, axis=1), stacked, preferred_element_type=f32)
         high, low = split(flat[:40])
-        start, lanes = 3072 + 768 * (f // 2), slice(128 * (f % 2), 128 * (f % 2) + 128)
+        start, lanes = 3456 + 768 * (f // 2), slice(128 * (f % 2), 128 * (f % 2) + 128)
         total = total + jnp.dot(
             jnp.concatenate([high, low, high], axis=1),
             table[start : start + 768, lanes],
@@ -263,7 +262,8 @@
     near_side[:64] = chosen
     near_side[64:, :128] = first
     near_side[64:, 128:] = second
-    store.wait()
+    for store in stores:
+        store.wait()
 
 
 def sides(near_side, far_side, axis):
@@ -305,7 +305,7 @@
     out[:, 1, 7] = partial[:, 1, 7] + from_high[:64].reshape(4, 2, 8, 256)
 
 
-def fourth_kernel(near_side, far_side, hold, sep, inner, sums, term):
+def right_side(near_side, far_side, hold):
     low_rows, high_rows = sides(near_side.at[:, 64:], far_side.at[64:], "pair")
     rows = []
     for vx in range(2):
@@ -315,18 +315,25 @@
             hold[8 * vx + 2 : 8 * vx + 3] + low_rows[4:5, lanes] + high_rows[0:1, lanes]
         )
     upright = jnp.transpose(jnp.concatenate(rows + rows, axis=0))
-    columns = [upright[:33, v : v + 1] for v in range(4)]
+    return [upright[:33, v : v + 1] for v in range(4)]
+
+
+def fourth_kernel(near_side, far_side, hold, sep, sums):
+    columns = right_side(near_side, far_side, hold)
     for at in range(8):
         lanes = slice(128 * at, 128 * at + 128)
         total = sum(columns[v] * sep[v // 2, v % 2, :, lanes] for v in range(4))
-        sums[at : at + 1] = jnp.sum(total, axis=0, keepdims=True)
+        sums[0, at : at + 1] = jnp.sum(total, axis=0, keepdims=True)
+    sums[1:] = jnp.broadcast_to(sums[0][None], (sums.shape[0] - 1, 8, 128))
+
+
+def inner_kernel(near_side, far_side, hold, inner, term):
+    columns = right_side(near_side, far_side, hold)
     total = sum(columns[v] * inner[v // 2, v % 2] for v in range(4))
     total = jnp.sum(total, axis=0, keepdims=True)
     for v in range(4):
-        term[v // 2, v % 2 : v % 2 + 1] = lax.dot_general(
-            total, inner[v // 2, v % 2], (((1,), (1,)), ((), ())),
-            precision=lax.Precision.HIGHEST, preferred_element_type=f32,
-        )
+        part = inner[v // 2, v % 2] * total
+        term[v // 2, v % 2 : v % 2 + 1] = jnp.sum(part, axis=1)[None]
 
 
 def fifth_kernel(partial, near_side, far_side, out):
@@ -343,14 +350,12 @@
 
 def last_kernel(arrived, sep, term, out):
     total = jnp.sum(arrived[...], axis=0)
-    ones = jnp.ones((1, 128), f32)
     for v in range(4):
-        spread_out = sum(
+        part = sum(
             sep[v // 2, v % 2, :, 128 * at : 128 * at + 128] * total[at : at + 1] for at in range(8)
         )
-        out[v // 2, v % 2 : v % 2 + 1] = term[v // 2, v % 2 : v % 2 + 1] + lax.dot_general(
-            ones, spread_out, (((1,), (1,)), ((), ())),
-            precision=lax.Precision.HIGHEST, preferred_element_type=f32,
+        out[v // 2, v % 2 : v % 2 + 1] = (
+            term[v // 2, v % 2 : v % 2 + 1] + jnp.sum(part, axis=1)[None]
         )
 
 
@@ -381,7 +386,7 @@
             pltpu.VMEM((4, 2, 8, 2, 8, 384), f32),
             pltpu.VMEM(fields.shape, f32),
             pltpu.SemaphoreType.DMA((5,)),
-            pltpu.SemaphoreType.DMA,
+            pltpu.SemaphoreType.DMA((2,)),
         ],
         compiler_params=pltpu.CompilerParams(vmem_limit_bytes=214 * 2**18),
     )(*arrays)
@@ -398,11 +403,6 @@
 def swapped(x, axis):
     count = lax.axis_size(axis)
     return moved(x, axis, lambda i: (i + (1 if i % 2 else count - 1)) % count)
-
-
-def scattered(parts, axis):
-    copies = call(spread_kernel, [(lax.axis_size(axis),) + parts.shape[1:]], [parts])[0]
-    return lax.all_to_all(copies, axis, 0, 0)
 
 
 def local(fields, sep_factor, local_factor):
@@ -417,13 +417,18 @@
     far_y = swapped(far_y, cross)
     near_y = lax.all_gather(near_y, "pair")
     partial = call(third_kernel, [fields.shape], [partial, from_low, from_high])[0]
-    sums, term = call(
-        fourth_kernel, [(8, 128), (2, 2, 33)], [near_y, far_y, hold, sep_factor, local_factor]
-    )
+    across = ("x",) + cross
+    along = ("z", "core")
+    sums = call(
+        fourth_kernel,
+        [(lax.axis_size(across), 8, 128)],
+        [near_y, far_y, hold, sep_factor],
+    )[0]
+    term = call(inner_kernel, [(2, 2, 33)], [near_y, far_y, hold, local_factor])[0]
     conv_rate = call(fifth_kernel, [fields.shape], [partial, near_y, far_y])[0]
-    sums = lax.all_gather(sums, "core")
-    sums = scattered(sums, ("x",) + cross)
-    sums = scattered(sums, "z")
+    sums = lax.all_to_all(sums, across, 0, 0)
+    sums = call(spread_kernel, [(lax.axis_size(along), 8, 128)], [sums])[0]
+    sums = lax.all_to_all(sums, along, 0, 0)
     pressure = call(last_kernel, [(2, 2, 33)], [sums, sep_factor, term])[0]
     return conv_rate, pressure
 

time: 73.3 us -> 71.8 us (0.980)
  the two profiles are of different devices: /device:TPU:8 before, /device:TPU:1 now
where the time goes in v2:
time: 71.8 us; the launch traced here: 71.5 us
  blocking collectives  31.9 us (44%)
  starting transfers between devices  18.5 us (26%)
  Pallas kernels  10.6 us (15%)
  waiting for transfers between devices  9.49 us (13%)
  between operations  0.75 us (1%)
    all_gather x1, blocking collectives, local(): near_side = lax.all_gather(near_side, 'core')  14.8 us
    all_to_all x1, blocking collectives, local(): sums = lax.all_to_all(sums, across, 0, 0)  13.3 us
    ppermute x2, starting transfers between devices, moved(): lax.ppermute(x, axis, [(i, target(i)) for i in range(lax.axis_size(axis))])  9.74 us
    all_to_all x1, waiting for transfers between devices, local(): sums = lax.all_to_all(sums, along, 0, 0)  9.48 us
    all_to_all x1, starting transfers between devices, local(): sums = lax.all_to_all(sums, along, 0, 0)  8.78 us
    pallas_call x1, Pallas kernels, first(): pl.pallas_call(first_kernel, out_shape=[jax.ShapeDtypeStruct(s, f32) for...  7.41 us
    all_gather x1, blocking collectives, local(): near_y = lax.all_gather(near_y, 'pair')  3.88 us
    pallas_call x7, Pallas kernels, call(): pl.pallas_call(kernel, out_shape=[jax.ShapeDtypeStruct(s, f32) for s in s...  3.17 us
  transfers between devices with their start and end apart: 3, of which 1 were waited for; matrix products, arithmetic and copies ran while one was open for 0% of the time, Pallas kernels for 2%

profile of v2, /device:TPU:1, one launch (start us, length us, event | category | flops | bytes accessed | tf_op | source)
XLA Modules:
  0.0 71.5 jit_solution(4344291402450088747)
XLA Ops:
  0.6 0.0 copy-start.1
  0.6 7.4 %shard_map.59 = (f32[4,2,8,2,8,256]{5,4,3,2,1,0:T(8,128)}, f32[72,256]{1,0:T(8,128)S(1)}, f32[72,256]{1,0:T(8,128)S(1)}, f32[64,256]{1,0:T(8,128)S(1)}, f32[64,256]{1,0:T(8,128)S(1)}, /*index=5*/f32[16,128]{1,0:T(8,128)S(1)}) custom-call(bf16[4,2,8,2,8,256]{5,4,3,2,1,0:T(8,128)(2,1)} %fields_far.1, bf16[4992,256]{1,0:T(8,128)(2,1)} %constant.2.clone.table_far), custom_call_target="tpu_custom_call" | custom-call | tf_op jit(solution)/shard_map/pallas_call | solution.py:378
  8.1 0.0 copy-start.2
  8.1 0.0 copy-start
  8.1 4.6 %collective-permute-start = (f32[72,256]{1,0:T(8,128)S(1)}, f32[72,256]{1,0:T(8,128)S(1)}, u32[]{:S(2)}, u32[]{:S(2)}) collective-permute-start(f32[72,256]{1,0:T(8,128)S(1)} %get-tuple-element.15), channel_id=1, source_target_pairs={{0,760},{8,16},{16,8},{24,32},{32,24},{40,48},{48,40},{56,64},{64,... | collective-permute-start | bytes 221192 | tf_op jit(solution)/shard_map/ppermute | solution.py:396
  12.7 14.8 %all-gather = f32[144,256]{1,0:T(8,128)S(1)} all-gather(f32[72,256]{1,0:T(8,128)S(1)} %get-tuple-element.14), channel_id=2, replica_groups=mesh['z'=12,'x'=4,'core'=2,'half'=4,'pair'=2] {'core'}, dimensions={0}, use_global_device_ids=true | all-gather | bytes 221184 | tf_op jit(solution)/shard_map/all_gather | solution.py:411
  27.5 0.0 collective-permute-done.far_side
  27.5 5.1 %collective-permute-start.1 = (f32[72,256]{1,0:T(8,128)S(1)}, f32[72,256]{1,0:T(8,128)S(1)}, u32[]{:S(2)}, u32[]{:S(2)}) collective-permute-start(f32[72,256]{1,0:T(8,128)S(1)} %get-tuple-element.22), channel_id=1, source_target_pairs={{0,7},{1,2},{2,1},{3,4},{4,3},{5,6},{6,5},{7,0},{8,15},{9,10},{10,... | collective-permute-start | bytes 221192 | tf_op jit(solution)/shard_map/ppermute | solution.py:396
  32.7 0.0 copy-done.1
  32.7 0.2 copy.6.sep
  32.9 3.9 %all-gather.1 = f32[144,256]{1,0:T(8,128)S(1)} all-gather(f32[72,256]{1,0:T(8,128)S(1)} %get-tuple-element.21), channel_id=3, replica_groups=mesh['z'=12,'x'=4,'core'=2,'half'=4,'pair'=2] {'pair'}, dimensions={0}, use_global_device_ids=true | all-gather | bytes 221184 | tf_op jit(solution)/shard_map/all_gather | solution.py:418
  36.7 0.0 collective-permute-done.1.far_side
  36.7 0.2 shard_map.63
  37.0 13.3 %all_to_all.10.parts = f32[32,8,128]{2,1,0:T(8,128)S(1)} all-to-all(f32[32,8,128]{2,1,0:T(8,128)S(1)} %shard_map.63), channel_id=1, replica_groups=mesh['z'=12,'x'=4,'core'=2,'half'=4,'pair'=2] {'x','half','pair'}, dimensions={0} | all-to-all | bytes 262144 | tf_op jit(solution)/shard_map/all_to_all | solution.py:429
  50.2 0.7 shard_map.64
  50.9 8.8 %all-to-all-start.1 = ((f32[24,8,128]{2,1,0:T(8,128)}), f32[24,8,128]{2,1,0:T(8,128)S(1)}, u32[]{:S(2)}, u32[]{:S(2)}) async-start(f32[24,8,128]{2,1,0:T(8,128)} %shard_map.64), calls=%async_computation.1 | async-start | bytes 196608 | tf_op jit(solution)/shard_map/all_to_all | solution.py:431
  59.7 0.0 copy-done.2
  59.7 0.0 copy-done
  59.7 0.1 shard_map.61.partial
  59.8 1.1 %shard_map.62 = f32[4,2,8,2,8,256]{5,4,3,2,1,0:T(8,128)} custom-call(f32[4,2,8,2,8,256]{5,4,3,2,1,0:T(8,128)S(1)} %shard_map.61.partial, f32[2,72,256]{2,1,0:T(8,128)S(1)} %bitcast.3, f32[72,256]{1,0:T(8,128)S(1)} %collective-permute-done.1.far_side), custom_call_target="tpu_custom_call" | custom-call | tf_op jit(solution)/shard_map/pallas_call | solution.py:364
  61.0 0.3 shard_map.65.term
  61.3 9.5 %all-to-all-done.1.arrived = f32[24,8,128]{2,1,0:T(8,128)S(1)} async-done(((f32[24,8,128]{2,1,0:T(8,128)}), f32[24,8,128]{2,1,0:T(8,128)S(1)}, u32[]{:S(2)}, u32[]{:S(2)}) %all-to-all-start.1) | async-done | bytes 98336 | tf_op jit(solution)/shard_map/all_to_all | solution.py:431
  70.8 0.7 %shard_map.66 = f32[2,2,33]{2,1,0:T(2,128)} custom-call(f32[24,8,128]{2,1,0:T(8,128)S(1)} %all-to-all-done.1.arrived, f32[2,2,33,1024]{3,2,1,0:T(8,128)S(1)} %copy.6.sep, f32[2,2,33]{2,1,0:T(2,128)S(1)} %shard_map.65.term), custom_call_target="tpu_custom_call" | custom-call | tf_op jit(solution)/shard_map/pallas_call | solution.py:364
  (2 shorter events, 0.1 us)
Async XLA Ops:
  0.6 32.0 %copy-start.1 = (f32[2,2,33,1024]{3,1,2,0:T(2,128)S(1)}, f32[2,2,33,1024]{3,1,2,0:T(2,128)}, u32[]{:S(2)}) copy-start(f32[2,2,33,1024]{3,1,2,0:T(2,128)} %param.5) | copy-start | bytes 1622020
  8.1 51.6 %copy-start.2 = (f32[2,2,33,132]{3,1,2,0:T(2,128)S(1)}, f32[2,2,33,132]{3,1,2,0:T(2,128)}, u32[]{:S(2)}) copy-start(f32[2,2,33,132]{3,1,2,0:T(2,128)} %param.6) | copy-start | bytes 209092
  8.1 51.7 %copy-start = (f32[4,2,8,2,8,256]{5,4,3,2,1,0:T(8,128)S(1)}, f32[4,2,8,2,8,256]{5,4,3,2,1,0:T(8,128)}, u32[]{:S(2)}) copy-start(f32[4,2,8,2,8,256]{5,4,3,2,1,0:T(8,128)} %get-tuple-element.13.partial) | copy-start | bytes 3145732
  8.1 19.4 %collective-permute-start = (f32[72,256]{1,0:T(8,128)S(1)}, f32[72,256]{1,0:T(8,128)S(1)}, u32[]{:S(2)}, u32[]{:S(2)}) collective-permute-start(f32[72,256]{1,0:T(8,128)S(1)} %get-tuple-element.15), channel_id=1, source_target_pairs={{0,760},{8,16},{16,8},{24,32},{32,24},{40,48},{48,40},{56,64},{64,... | collective-permute-start | bytes 221192 | tf_op jit(solution)/shard_map/ppermute | solution.py:396
  27.5 9.2 %collective-permute-start.1 = (f32[72,256]{1,0:T(8,128)S(1)}, f32[72,256]{1,0:T(8,128)S(1)}, u32[]{:S(2)}, u32[]{:S(2)}) collective-permute-start(f32[72,256]{1,0:T(8,128)S(1)} %get-tuple-element.22), channel_id=1, source_target_pairs={{0,7},{1,2},{2,1},{3,4},{4,3},{5,6},{6,5},{7,0},{8,15},{9,10},{10,... | collective-permute-start | bytes 221192 | tf_op jit(solution)/shard_map/ppermute | solution.py:396
  50.9 19.8 %all-to-all-start.1 = ((f32[24,8,128]{2,1,0:T(8,128)}), f32[24,8,128]{2,1,0:T(8,128)S(1)}, u32[]{:S(2)}, u32[]{:S(2)}) async-start(f32[24,8,128]{2,1,0:T(8,128)} %shard_map.64), calls=%async_computation.1 | async-start | bytes 196608 | tf_op jit(solution)/shard_map/all_to_all | solution.py:431

commit v3 on v2

--- a/solution.py
+++ b/solution.py
@@ -275,7 +275,7 @@
 
 
 def second_kernel(
-    near_side, far_side, low_y, high_y, hold, near_out, far_out, hold_out, from_low, from_high
+    near_side, far_side, low_y, high_y, hold, sep, near_out, far_out, hold_out, from_low, from_high
 ):
     from_low[...], from_high[...] = sides(near_side, far_side, "core")
     even = lax.axis_index("pair") == 0
@@ -412,13 +412,13 @@
     near_y, far_y, hold, from_low, from_high = call(
         second_kernel,
         [(72, 256), (72, 256), (16, 128), (72, 256), (72, 256)],
-        [near_side, far_side, low_y, high_y, hold],
+        [near_side, far_side, low_y, high_y, hold, sep_factor],
     )
     far_y = swapped(far_y, cross)
     near_y = lax.all_gather(near_y, "pair")
     partial = call(third_kernel, [fields.shape], [partial, from_low, from_high])[0]
-    across = ("x",) + cross
-    along = ("z", "core")
+    across = ("x", "pair", "half")
+    along = ("core", "z")
     sums = call(
         fourth_kernel,
         [(lax.axis_size(across), 8, 128)],

time: 71.8 us -> 71.1 us (level)
  no operation moved by 1% of the time
where the time goes in v3:
time: 71.1 us; the launch traced here: 70.4 us
  blocking collectives  31.9 us (45%)
  starting transfers between devices  17.9 us (25%)
  Pallas kernels  10.6 us (15%)
  waiting for transfers between devices  9.14 us (13%)
  between operations  0.75 us (1%)
    all_gather x1, blocking collectives, local(): near_side = lax.all_gather(near_side, 'core')  14.8 us
    all_to_all x1, blocking collectives, local(): sums = lax.all_to_all(sums, across, 0, 0)  13.2 us
    ppermute x2, starting transfers between devices, moved(): lax.ppermute(x, axis, [(i, target(i)) for i in range(lax.axis_size(axis))])  9.74 us
    all_to_all x1, waiting for transfers between devices, local(): sums = lax.all_to_all(sums, along, 0, 0)  9.13 us
    all_to_all x1, starting transfers between devices, local(): sums = lax.all_to_all(sums, along, 0, 0)  8.15 us
    pallas_call x1, Pallas kernels, first(): pl.pallas_call(first_kernel, out_shape=[jax.ShapeDtypeStruct(s, f32) for...  7.41 us
    all_gather x1, blocking collectives, local(): near_y = lax.all_gather(near_y, 'pair')  3.88 us
    pallas_call x7, Pallas kernels, call(): pl.pallas_call(kernel, out_shape=[jax.ShapeDtypeStruct(s, f32) for s in s...  3.18 us
  transfers between devices with their start and end apart: 3, of which 1 were waited for; matrix products, arithmetic and copies ran while one was open for 0% of the time, Pallas kernels for 2%

profile of v3, /device:TPU:1, one launch (start us, length us, event | category | flops | bytes accessed | tf_op | source)
XLA Modules:
  0.0 70.4 jit_solution(4772452741077689747)
XLA Ops:
  0.6 0.0 copy-start.1
  0.6 7.4 %shard_map.59 = (f32[4,2,8,2,8,256]{5,4,3,2,1,0:T(8,128)}, f32[72,256]{1,0:T(8,128)S(1)}, f32[72,256]{1,0:T(8,128)S(1)}, f32[64,256]{1,0:T(8,128)S(1)}, f32[64,256]{1,0:T(8,128)S(1)}, /*index=5*/f32[16,128]{1,0:T(8,128)S(1)}) custom-call(bf16[4,2,8,2,8,256]{5,4,3,2,1,0:T(8,128)(2,1)} %fields_far.1, bf16[4992,256]{1,0:T(8,128)(2,1)} %constant.2.clone.table_far), custom_call_target="tpu_custom_call" | custom-call | tf_op jit(solution)/shard_map/pallas_call | solution.py:378
  8.1 0.0 copy-start.2
  8.1 0.0 copy-start
  8.1 4.6 %collective-permute-start = (f32[72,256]{1,0:T(8,128)S(1)}, f32[72,256]{1,0:T(8,128)S(1)}, u32[]{:S(2)}, u32[]{:S(2)}) collective-permute-start(f32[72,256]{1,0:T(8,128)S(1)} %get-tuple-element.15), channel_id=1, source_target_pairs={{0,760},{8,16},{16,8},{24,32},{32,24},{40,48},{48,40},{56,64},{64,... | collective-permute-start | bytes 221192 | tf_op jit(solution)/shard_map/ppermute | solution.py:396
  12.7 0.0 copy-done.1
  12.7 0.2 copy.6.sep
  12.9 14.8 %all-gather = f32[144,256]{1,0:T(8,128)S(1)} all-gather(f32[72,256]{1,0:T(8,128)S(1)} %get-tuple-element.14), channel_id=2, replica_groups=mesh['z'=12,'x'=4,'core'=2,'half'=4,'pair'=2] {'core'}, dimensions={0}, use_global_device_ids=true | all-gather | bytes 221184 | tf_op jit(solution)/shard_map/all_gather | solution.py:411
  27.7 0.0 collective-permute-done.far_side
  27.7 5.1 %collective-permute-start.1 = (f32[72,256]{1,0:T(8,128)S(1)}, f32[72,256]{1,0:T(8,128)S(1)}, u32[]{:S(2)}, u32[]{:S(2)}) collective-permute-start(f32[72,256]{1,0:T(8,128)S(1)} %get-tuple-element.22), channel_id=1, source_target_pairs={{0,7},{1,2},{2,1},{3,4},{4,3},{5,6},{6,5},{7,0},{8,15},{9,10},{10,... | collective-permute-start | bytes 221192 | tf_op jit(solution)/shard_map/ppermute | solution.py:396
  32.9 3.9 %all-gather.1 = f32[144,256]{1,0:T(8,128)S(1)} all-gather(f32[72,256]{1,0:T(8,128)S(1)} %get-tuple-element.21), channel_id=3, replica_groups=mesh['z'=12,'x'=4,'core'=2,'half'=4,'pair'=2] {'pair'}, dimensions={0}, use_global_device_ids=true | all-gather | bytes 221184 | tf_op jit(solution)/shard_map/all_gather | solution.py:418
  36.7 0.0 collective-permute-done.1.far_side
  36.7 0.2 shard_map.63
  37.0 13.2 %all_to_all.10.parts = f32[32,8,128]{2,1,0:T(8,128)S(1)} all-to-all(f32[32,8,128]{2,1,0:T(8,128)S(1)} %shard_map.63), channel_id=1, replica_groups=mesh['z'=12,'x'=4,'core'=2,'half'=4,'pair'=2] {'x','pair','half'}, dimensions={0} | all-to-all | bytes 262144 | tf_op jit(solution)/shard_map/all_to_all | solution.py:429
  50.2 0.7 shard_map.64
  50.9 8.1 %all-to-all-start.1 = ((f32[24,8,128]{2,1,0:T(8,128)}), f32[24,8,128]{2,1,0:T(8,128)S(1)}, u32[]{:S(2)}, u32[]{:S(2)}) async-start(f32[24,8,128]{2,1,0:T(8,128)} %shard_map.64), calls=%async_computation.1 | async-start | bytes 196608 | tf_op jit(solution)/shard_map/all_to_all | solution.py:431
  59.0 0.0 copy-done.2
  59.0 0.0 copy-done
  59.1 0.1 shard_map.61.partial
  59.1 0.3 shard_map.65.term
  59.4 1.1 %shard_map.62 = f32[4,2,8,2,8,256]{5,4,3,2,1,0:T(8,128)} custom-call(f32[4,2,8,2,8,256]{5,4,3,2,1,0:T(8,128)S(1)} %shard_map.61.partial, f32[2,72,256]{2,1,0:T(8,128)S(1)} %bitcast.4, f32[72,256]{1,0:T(8,128)S(1)} %collective-permute-done.1.far_side), custom_call_target="tpu_custom_call" | custom-call | tf_op jit(solution)/shard_map/pallas_call | solution.py:364
  60.6 9.1 %all-to-all-done.1.arrived = f32[24,8,128]{2,1,0:T(8,128)S(1)} async-done(((f32[24,8,128]{2,1,0:T(8,128)}), f32[24,8,128]{2,1,0:T(8,128)S(1)}, u32[]{:S(2)}, u32[]{:S(2)}) %all-to-all-start.1) | async-done | bytes 98336 | tf_op jit(solution)/shard_map/all_to_all | solution.py:431
  69.7 0.7 %shard_map.66 = f32[2,2,33]{2,1,0:T(2,128)} custom-call(f32[24,8,128]{2,1,0:T(8,128)S(1)} %all-to-all-done.1.arrived, f32[2,2,33,1024]{3,2,1,0:T(8,128)S(1)} %copy.6.sep, f32[2,2,33]{2,1,0:T(2,128)S(1)} %shard_map.65.term), custom_call_target="tpu_custom_call" | custom-call | tf_op jit(solution)/shard_map/pallas_call | solution.py:364
  (2 shorter events, 0.1 us)
Async XLA Ops:
  0.6 12.1 %copy-start.1 = (f32[2,2,33,1024]{3,1,2,0:T(2,128)S(1)}, f32[2,2,33,1024]{3,1,2,0:T(2,128)}, u32[]{:S(2)}) copy-start(f32[2,2,33,1024]{3,1,2,0:T(2,128)} %param.5) | copy-start | bytes 1622020
  8.1 51.0 %copy-start.2 = (f32[2,2,33,132]{3,1,2,0:T(2,128)S(1)}, f32[2,2,33,132]{3,1,2,0:T(2,128)}, u32[]{:S(2)}) copy-start(f32[2,2,33,132]{3,1,2,0:T(2,128)} %param.6) | copy-start | bytes 209092
  8.1 51.0 %copy-start = (f32[4,2,8,2,8,256]{5,4,3,2,1,0:T(8,128)S(1)}, f32[4,2,8,2,8,256]{5,4,3,2,1,0:T(8,128)}, u32[]{:S(2)}) copy-start(f32[4,2,8,2,8,256]{5,4,3,2,1,0:T(8,128)} %get-tuple-element.13.partial) | copy-start | bytes 3145732
  8.1 19.6 %collective-permute-start = (f32[72,256]{1,0:T(8,128)S(1)}, f32[72,256]{1,0:T(8,128)S(1)}, u32[]{:S(2)}, u32[]{:S(2)}) collective-permute-start(f32[72,256]{1,0:T(8,128)S(1)} %get-tuple-element.15), channel_id=1, source_target_pairs={{0,760},{8,16},{16,8},{24,32},{32,24},{40,48},{48,40},{56,64},{64,... | collective-permute-start | bytes 221192 | tf_op jit(solution)/shard_map/ppermute | solution.py:396
  27.7 9.0 %collective-permute-start.1 = (f32[72,256]{1,0:T(8,128)S(1)}, f32[72,256]{1,0:T(8,128)S(1)}, u32[]{:S(2)}, u32[]{:S(2)}) collective-permute-start(f32[72,256]{1,0:T(8,128)S(1)} %get-tuple-element.22), channel_id=1, source_target_pairs={{0,7},{1,2},{2,1},{3,4},{4,3},{5,6},{6,5},{7,0},{8,15},{9,10},{10,... | collective-permute-start | bytes 221192 | tf_op jit(solution)/shard_map/ppermute | solution.py:396
  50.9 18.9 %all-to-all-start.1 = ((f32[24,8,128]{2,1,0:T(8,128)}), f32[24,8,128]{2,1,0:T(8,128)S(1)}, u32[]{:S(2)}, u32[]{:S(2)}) async-start(f32[24,8,128]{2,1,0:T(8,128)} %shard_map.64), calls=%async_computation.1 | async-start | bytes 196608 | tf_op jit(solution)/shard_map/all_to_all | solution.py:431

commit v4 on v3

--- a/solution.py
+++ b/solution.py
@@ -396,7 +396,7 @@
     return lax.ppermute(x, axis, [(i, target(i)) for i in range(lax.axis_size(axis))])
 
 
-slab = ("z", "x", "core")
+slab = ("high", "low", "x", "core")
 cross = ("half", "pair")
 
 
@@ -418,7 +418,7 @@
     near_y = lax.all_gather(near_y, "pair")
     partial = call(third_kernel, [fields.shape], [partial, from_low, from_high])[0]
     across = ("x", "pair", "half")
-    along = ("core", "z")
+    along = ("low", "core", "high")
     sums = call(
         fourth_kernel,
         [(lax.axis_size(across), 8, 128)],
@@ -434,7 +434,7 @@
 
 
 def solution(mesh):
-    fine = Mesh(mesh.devices.reshape(12, 4, 2, 4, 2), slab + cross)
+    fine = Mesh(mesh.devices.reshape(3, 4, 4, 2, 4, 2), slab + cross)
     return jax.shard_map(
         local,
         mesh=fine,

time: 71.1 us -> 71.2 us (level)
  no operation moved by 1% of the time
where the time goes in v4:
time: 71.2 us; the launch traced here: 70.9 us
  blocking collectives  31.9 us (45%)
  starting transfers between devices  17.9 us (25%)
  Pallas kernels  10.6 us (15%)
  waiting for transfers between devices  9.63 us (14%)
  between operations  0.75 us (1%)
    all_gather x1, blocking collectives, local(): near_side = lax.all_gather(near_side, 'core')  14.8 us
    all_to_all x1, blocking collectives, local(): sums = lax.all_to_all(sums, across, 0, 0)  13.2 us
    ppermute x2, starting transfers between devices, moved(): lax.ppermute(x, axis, [(i, target(i)) for i in range(lax.axis_size(axis))])  9.74 us
    all_to_all x1, waiting for transfers between devices, local(): sums = lax.all_to_all(sums, along, 0, 0)  9.62 us
    all_to_all x1, starting transfers between devices, local(): sums = lax.all_to_all(sums, along, 0, 0)  8.14 us
    pallas_call x1, Pallas kernels, first(): pl.pallas_call(first_kernel, out_shape=[jax.ShapeDtypeStruct(s, f32) for...  7.41 us
    all_gather x1, blocking collectives, local(): near_y = lax.all_gather(near_y, 'pair')  3.88 us
    pallas_call x7, Pallas kernels, call(): pl.pallas_call(kernel, out_shape=[jax.ShapeDtypeStruct(s, f32) for s in s...  3.18 us
  transfers between devices with their start and end apart: 3, of which 1 were waited for; matrix products, arithmetic and copies ran while one was open for 0% of the time, Pallas kernels for 2%

profile of v4, /device:TPU:1, one launch (start us, length us, event | category | flops | bytes accessed | tf_op | source)
XLA Modules:
  0.0 70.9 jit_solution(18249897790504323348)
XLA Ops:
  0.6 0.0 copy-start.1
  0.6 7.4 %shard_map.59 = (f32[4,2,8,2,8,256]{5,4,3,2,1,0:T(8,128)}, f32[72,256]{1,0:T(8,128)S(1)}, f32[72,256]{1,0:T(8,128)S(1)}, f32[64,256]{1,0:T(8,128)S(1)}, f32[64,256]{1,0:T(8,128)S(1)}, /*index=5*/f32[16,128]{1,0:T(8,128)S(1)}) custom-call(bf16[4,2,8,2,8,256]{5,4,3,2,1,0:T(8,128)(2,1)} %fields_far.1, bf16[4992,256]{1,0:T(8,128)(2,1)} %constant.2.clone.table_far), custom_call_target="tpu_custom_call" | custom-call | tf_op jit(solution)/shard_map/pallas_call | solution.py:378
  8.1 0.0 copy-start.2
  8.1 0.0 copy-start
  8.1 4.6 %collective-permute-start = (f32[72,256]{1,0:T(8,128)S(1)}, f32[72,256]{1,0:T(8,128)S(1)}, u32[]{:S(2)}, u32[]{:S(2)}) collective-permute-start(f32[72,256]{1,0:T(8,128)S(1)} %get-tuple-element.15), channel_id=1, source_target_pairs={{0,760},{8,16},{16,8},{24,32},{32,24},{40,48},{48,40},{56,64},{64,... | collective-permute-start | bytes 221192 | tf_op jit(solution)/shard_map/ppermute | solution.py:396
  12.7 0.0 copy-done.1
  12.7 0.2 copy.6.sep
  12.9 14.8 %all-gather = f32[144,256]{1,0:T(8,128)S(1)} all-gather(f32[72,256]{1,0:T(8,128)S(1)} %get-tuple-element.14), channel_id=2, replica_groups=mesh['high'=3,'low'=4,'x'=4,'core'=2,'half'=4,'pair'=2] {'core'}, dimensions={0}, use_global_device_ids=true | all-gather | bytes 221184 | tf_op jit(solution)/shard_map/all_gather | solution.py:411
  27.7 0.0 collective-permute-done.far_side
  27.7 5.1 %collective-permute-start.1 = (f32[72,256]{1,0:T(8,128)S(1)}, f32[72,256]{1,0:T(8,128)S(1)}, u32[]{:S(2)}, u32[]{:S(2)}) collective-permute-start(f32[72,256]{1,0:T(8,128)S(1)} %get-tuple-element.22), channel_id=1, source_target_pairs={{0,7},{1,2},{2,1},{3,4},{4,3},{5,6},{6,5},{7,0},{8,15},{9,10},{10,... | collective-permute-start | bytes 221192 | tf_op jit(solution)/shard_map/ppermute | solution.py:396
  32.9 3.9 %all-gather.1 = f32[144,256]{1,0:T(8,128)S(1)} all-gather(f32[72,256]{1,0:T(8,128)S(1)} %get-tuple-element.21), channel_id=3, replica_groups=mesh['high'=3,'low'=4,'x'=4,'core'=2,'half'=4,'pair'=2] {'pair'}, dimensions={0}, use_global_device_ids=true | all-gather | bytes 221184 | tf_op jit(solution)/shard_map/all_gather | solution.py:418
  36.7 0.0 collective-permute-done.1.far_side
  36.7 0.2 shard_map.63
  37.0 13.2 %all_to_all.10.parts = f32[32,8,128]{2,1,0:T(8,128)S(1)} all-to-all(f32[32,8,128]{2,1,0:T(8,128)S(1)} %shard_map.63), channel_id=1, replica_groups=mesh['high'=3,'low'=4,'x'=4,'core'=2,'half'=4,'pair'=2] {'x','pair','half'}, dimensions={0} | all-to-all | bytes 262144 | tf_op jit(solution)/shard_map/all_to_all | solution.py:429
  50.2 0.7 shard_map.64
  50.9 8.1 %all-to-all-start.1 = ((f32[24,8,128]{2,1,0:T(8,128)}), f32[24,8,128]{2,1,0:T(8,128)S(1)}, u32[]{:S(2)}, u32[]{:S(2)}) async-start(f32[24,8,128]{2,1,0:T(8,128)} %shard_map.64), calls=%async_computation.1 | async-start | bytes 196608 | tf_op jit(solution)/shard_map/all_to_all | solution.py:431
  59.0 0.0 copy-done.2
  59.0 0.0 copy-done
  59.1 0.1 shard_map.61.partial
  59.1 0.3 shard_map.65.term
  59.4 1.1 %shard_map.62 = f32[4,2,8,2,8,256]{5,4,3,2,1,0:T(8,128)} custom-call(f32[4,2,8,2,8,256]{5,4,3,2,1,0:T(8,128)S(1)} %shard_map.61.partial, f32[2,72,256]{2,1,0:T(8,128)S(1)} %bitcast.4, f32[72,256]{1,0:T(8,128)S(1)} %collective-permute-done.1.far_side), custom_call_target="tpu_custom_call" | custom-call | tf_op jit(solution)/shard_map/pallas_call | solution.py:364
  60.6 9.6 %all-to-all-done.1.arrived = f32[24,8,128]{2,1,0:T(8,128)S(1)} async-done(((f32[24,8,128]{2,1,0:T(8,128)}), f32[24,8,128]{2,1,0:T(8,128)S(1)}, u32[]{:S(2)}, u32[]{:S(2)}) %all-to-all-start.1) | async-done | bytes 98336 | tf_op jit(solution)/shard_map/all_to_all | solution.py:431
  70.2 0.7 %shard_map.66 = f32[2,2,33]{2,1,0:T(2,128)} custom-call(f32[24,8,128]{2,1,0:T(8,128)S(1)} %all-to-all-done.1.arrived, f32[2,2,33,1024]{3,2,1,0:T(8,128)S(1)} %copy.6.sep, f32[2,2,33]{2,1,0:T(2,128)S(1)} %shard_map.65.term), custom_call_target="tpu_custom_call" | custom-call | tf_op jit(solution)/shard_map/pallas_call | solution.py:364
  (2 shorter events, 0.1 us)
Async XLA Ops:
  0.6 12.1 %copy-start.1 = (f32[2,2,33,1024]{3,1,2,0:T(2,128)S(1)}, f32[2,2,33,1024]{3,1,2,0:T(2,128)}, u32[]{:S(2)}) copy-start(f32[2,2,33,1024]{3,1,2,0:T(2,128)} %param.5) | copy-start | bytes 1622020
  8.1 51.0 %copy-start.2 = (f32[2,2,33,132]{3,1,2,0:T(2,128)S(1)}, f32[2,2,33,132]{3,1,2,0:T(2,128)}, u32[]{:S(2)}) copy-start(f32[2,2,33,132]{3,1,2,0:T(2,128)} %param.6) | copy-start | bytes 209092
  8.1 51.0 %copy-start = (f32[4,2,8,2,8,256]{5,4,3,2,1,0:T(8,128)S(1)}, f32[4,2,8,2,8,256]{5,4,3,2,1,0:T(8,128)}, u32[]{:S(2)}) copy-start(f32[4,2,8,2,8,256]{5,4,3,2,1,0:T(8,128)} %get-tuple-element.13.partial) | copy-start | bytes 3145732
  8.1 19.6 %collective-permute-start = (f32[72,256]{1,0:T(8,128)S(1)}, f32[72,256]{1,0:T(8,128)S(1)}, u32[]{:S(2)}, u32[]{:S(2)}) collective-permute-start(f32[72,256]{1,0:T(8,128)S(1)} %get-tuple-element.15), channel_id=1, source_target_pairs={{0,760},{8,16},{16,8},{24,32},{32,24},{40,48},{48,40},{56,64},{64,... | collective-permute-start | bytes 221192 | tf_op jit(solution)/shard_map/ppermute | solution.py:396
  27.7 9.0 %collective-permute-start.1 = (f32[72,256]{1,0:T(8,128)S(1)}, f32[72,256]{1,0:T(8,128)S(1)}, u32[]{:S(2)}, u32[]{:S(2)}) collective-permute-start(f32[72,256]{1,0:T(8,128)S(1)} %get-tuple-element.22), channel_id=1, source_target_pairs={{0,7},{1,2},{2,1},{3,4},{4,3},{5,6},{6,5},{7,0},{8,15},{9,10},{10,... | collective-permute-start | bytes 221192 | tf_op jit(solution)/shard_map/ppermute | solution.py:396
  50.9 19.3 %all-to-all-start.1 = ((f32[24,8,128]{2,1,0:T(8,128)}), f32[24,8,128]{2,1,0:T(8,128)S(1)}, u32[]{:S(2)}, u32[]{:S(2)}) async-start(f32[24,8,128]{2,1,0:T(8,128)} %shard_map.64), calls=%async_computation.1 | async-start | bytes 196608 | tf_op jit(solution)/shard_map/all_to_all | solution.py:431

commit v5 on v4

--- a/solution.py
+++ b/solution.py
@@ -407,6 +407,9 @@
 
 def local(fields, sep_factor, local_factor):
     partial, near_side, far_side, low_y, high_y, hold = first(fields)
+    far_side, sep_factor, local_factor = lax.optimization_barrier(
+        (far_side, sep_factor, local_factor)
+    )
     far_side = swapped(far_side, slab)
     near_side = lax.all_gather(near_side, "core")
     near_y, far_y, hold, from_low, from_high = call(

time: 71.2 us -> 71.2 us (level)
  no operation moved by 1% of the time
where the time goes in v5:
time: 71.2 us; the launch traced here: 70.9 us
  blocking collectives  31.9 us (45%)
  starting transfers between devices  17.9 us (25%)
  Pallas kernels  10.6 us (15%)
  waiting for transfers between devices  9.63 us (14%)
  between operations  0.75 us (1%)
    all_gather x1, blocking collectives, local(): near_side = lax.all_gather(near_side, 'core')  14.8 us
    all_to_all x1, blocking collectives, local(): sums = lax.all_to_all(sums, across, 0, 0)  13.2 us
    ppermute x2, starting transfers between devices, moved(): lax.ppermute(x, axis, [(i, target(i)) for i in range(lax.axis_size(axis))])  9.74 us
    all_to_all x1, waiting for transfers between devices, local(): sums = lax.all_to_all(sums, along, 0, 0)  9.62 us
    all_to_all x1, starting transfers between devices, local(): sums = lax.all_to_all(sums, along, 0, 0)  8.14 us
    pallas_call x1, Pallas kernels, first(): pl.pallas_call(first_kernel, out_shape=[jax.ShapeDtypeStruct(s, f32) for...  7.41 us
    all_gather x1, blocking collectives, local(): near_y = lax.all_gather(near_y, 'pair')  3.88 us
    pallas_call x7, Pallas kernels, call(): pl.pallas_call(kernel, out_shape=[jax.ShapeDtypeStruct(s, f32) for s in s...  3.18 us
  transfers between devices with their start and end apart: 3, of which 1 were waited for; matrix products, arithmetic and copies ran while one was open for 0% of the time, Pallas kernels for 2%

profile of v5, /device:TPU:1, one launch (start us, length us, event | category | flops | bytes accessed | tf_op | source)
XLA Modules:
  0.0 70.9 jit_solution(18249897790504323348)
XLA Ops:
  0.6 0.0 copy-start.1
  0.6 7.4 %shard_map.59 = (f32[4,2,8,2,8,256]{5,4,3,2,1,0:T(8,128)}, f32[72,256]{1,0:T(8,128)S(1)}, f32[72,256]{1,0:T(8,128)S(1)}, f32[64,256]{1,0:T(8,128)S(1)}, f32[64,256]{1,0:T(8,128)S(1)}, /*index=5*/f32[16,128]{1,0:T(8,128)S(1)}) custom-call(bf16[4,2,8,2,8,256]{5,4,3,2,1,0:T(8,128)(2,1)} %fields_far.1, bf16[4992,256]{1,0:T(8,128)(2,1)} %constant.2.clone.table_far), custom_call_target="tpu_custom_call" | custom-call | tf_op jit(solution)/shard_map/pallas_call | solution.py:378
  8.1 0.0 copy-start.2
  8.1 0.0 copy-start
  8.1 4.6 %collective-permute-start = (f32[72,256]{1,0:T(8,128)S(1)}, f32[72,256]{1,0:T(8,128)S(1)}, u32[]{:S(2)}, u32[]{:S(2)}) collective-permute-start(f32[72,256]{1,0:T(8,128)S(1)} %get-tuple-element.19), channel_id=1, source_target_pairs={{0,760},{8,16},{16,8},{24,32},{32,24},{40,48},{48,40},{56,64},{64,... | collective-permute-start | bytes 221192 | tf_op jit(solution)/shard_map/ppermute | solution.py:396
  12.7 0.0 copy-done.1
  12.7 0.2 copy.6.sep
  12.9 14.8 %all-gather = f32[144,256]{1,0:T(8,128)S(1)} all-gather(f32[72,256]{1,0:T(8,128)S(1)} %get-tuple-element.17), channel_id=2, replica_groups=mesh['high'=3,'low'=4,'x'=4,'core'=2,'half'=4,'pair'=2] {'core'}, dimensions={0}, use_global_device_ids=true | all-gather | bytes 221184 | tf_op jit(solution)/shard_map/all_gather | solution.py:414
  27.7 0.0 collective-permute-done.far_side
  27.7 5.1 %collective-permute-start.1 = (f32[72,256]{1,0:T(8,128)S(1)}, f32[72,256]{1,0:T(8,128)S(1)}, u32[]{:S(2)}, u32[]{:S(2)}) collective-permute-start(f32[72,256]{1,0:T(8,128)S(1)} %get-tuple-element.27), channel_id=1, source_target_pairs={{0,7},{1,2},{2,1},{3,4},{4,3},{5,6},{6,5},{7,0},{8,15},{9,10},{10,... | collective-permute-start | bytes 221192 | tf_op jit(solution)/shard_map/ppermute | solution.py:396
  32.9 3.9 %all-gather.1 = f32[144,256]{1,0:T(8,128)S(1)} all-gather(f32[72,256]{1,0:T(8,128)S(1)} %get-tuple-element.26), channel_id=3, replica_groups=mesh['high'=3,'low'=4,'x'=4,'core'=2,'half'=4,'pair'=2] {'pair'}, dimensions={0}, use_global_device_ids=true | all-gather | bytes 221184 | tf_op jit(solution)/shard_map/all_gather | solution.py:421
  36.7 0.0 collective-permute-done.1.far_side
  36.7 0.2 shard_map.63
  37.0 13.2 %all_to_all.10.parts = f32[32,8,128]{2,1,0:T(8,128)S(1)} all-to-all(f32[32,8,128]{2,1,0:T(8,128)S(1)} %shard_map.63), channel_id=1, replica_groups=mesh['high'=3,'low'=4,'x'=4,'core'=2,'half'=4,'pair'=2] {'x','pair','half'}, dimensions={0} | all-to-all | bytes 262144 | tf_op jit(solution)/shard_map/all_to_all | solution.py:432
  50.2 0.7 shard_map.64
  50.9 8.1 %all-to-all-start.1 = ((f32[24,8,128]{2,1,0:T(8,128)}), f32[24,8,128]{2,1,0:T(8,128)S(1)}, u32[]{:S(2)}, u32[]{:S(2)}) async-start(f32[24,8,128]{2,1,0:T(8,128)} %shard_map.64), calls=%async_computation.1 | async-start | bytes 196608 | tf_op jit(solution)/shard_map/all_to_all | solution.py:434
  59.0 0.0 copy-done.2
  59.0 0.0 copy-done
  59.1 0.1 shard_map.61.partial
  59.1 0.3 shard_map.65.term
  59.4 1.1 %shard_map.62 = f32[4,2,8,2,8,256]{5,4,3,2,1,0:T(8,128)} custom-call(f32[4,2,8,2,8,256]{5,4,3,2,1,0:T(8,128)S(1)} %shard_map.61.partial, f32[2,72,256]{2,1,0:T(8,128)S(1)} %bitcast.4, f32[72,256]{1,0:T(8,128)S(1)} %collective-permute-done.1.far_side), custom_call_target="tpu_custom_call" | custom-call | tf_op jit(solution)/shard_map/pallas_call | solution.py:364
  60.6 9.6 %all-to-all-done.1.arrived = f32[24,8,128]{2,1,0:T(8,128)S(1)} async-done(((f32[24,8,128]{2,1,0:T(8,128)}), f32[24,8,128]{2,1,0:T(8,128)S(1)}, u32[]{:S(2)}, u32[]{:S(2)}) %all-to-all-start.1) | async-done | bytes 98336 | tf_op jit(solution)/shard_map/all_to_all | solution.py:434
  70.2 0.7 %shard_map.66 = f32[2,2,33]{2,1,0:T(2,128)} custom-call(f32[24,8,128]{2,1,0:T(8,128)S(1)} %all-to-all-done.1.arrived, f32[2,2,33,1024]{3,2,1,0:T(8,128)S(1)} %copy.6.sep, f32[2,2,33]{2,1,0:T(2,128)S(1)} %shard_map.65.term), custom_call_target="tpu_custom_call" | custom-call | tf_op jit(solution)/shard_map/pallas_call | solution.py:364
  (2 shorter events, 0.1 us)
Async XLA Ops:
  0.6 12.1 %copy-start.1 = (f32[2,2,33,1024]{3,1,2,0:T(2,128)S(1)}, f32[2,2,33,1024]{3,1,2,0:T(2,128)}, u32[]{:S(2)}) copy-start(f32[2,2,33,1024]{3,1,2,0:T(2,128)} %param.5) | copy-start | bytes 1622020
  8.1 51.0 %copy-start.2 = (f32[2,2,33,132]{3,1,2,0:T(2,128)S(1)}, f32[2,2,33,132]{3,1,2,0:T(2,128)}, u32[]{:S(2)}) copy-start(f32[2,2,33,132]{3,1,2,0:T(2,128)} %param.6) | copy-start | bytes 209092
  8.1 51.0 %copy-start = (f32[4,2,8,2,8,256]{5,4,3,2,1,0:T(8,128)S(1)}, f32[4,2,8,2,8,256]{5,4,3,2,1,0:T(8,128)}, u32[]{:S(2)}) copy-start(f32[4,2,8,2,8,256]{5,4,3,2,1,0:T(8,128)} %get-tuple-element.16.partial) | copy-start | bytes 3145732
  8.1 19.6 %collective-permute-start = (f32[72,256]{1,0:T(8,128)S(1)}, f32[72,256]{1,0:T(8,128)S(1)}, u32[]{:S(2)}, u32[]{:S(2)}) collective-permute-start(f32[72,256]{1,0:T(8,128)S(1)} %get-tuple-element.19), channel_id=1, source_target_pairs={{0,760},{8,16},{16,8},{24,32},{32,24},{40,48},{48,40},{56,64},{64,... | collective-permute-start | bytes 221192 | tf_op jit(solution)/shard_map/ppermute | solution.py:396
  27.7 9.0 %collective-permute-start.1 = (f32[72,256]{1,0:T(8,128)S(1)}, f32[72,256]{1,0:T(8,128)S(1)}, u32[]{:S(2)}, u32[]{:S(2)}) collective-permute-start(f32[72,256]{1,0:T(8,128)S(1)} %get-tuple-element.27), channel_id=1, source_target_pairs={{0,7},{1,2},{2,1},{3,4},{4,3},{5,6},{6,5},{7,0},{8,15},{9,10},{10,... | collective-permute-start | bytes 221192 | tf_op jit(solution)/shard_map/ppermute | solution.py:396
  50.9 19.3 %all-to-all-start.1 = ((f32[24,8,128]{2,1,0:T(8,128)}), f32[24,8,128]{2,1,0:T(8,128)S(1)}, u32[]{:S(2)}, u32[]{:S(2)}) async-start(f32[24,8,128]{2,1,0:T(8,128)} %shard_map.64), calls=%async_computation.1 | async-start | bytes 196608 | tf_op jit(solution)/shard_map/all_to_all | solution.py:434
